TPU v7x, 32 devices: a whole 2x2x4 slice. The times are simulated.
32 devices in a mesh: test: 4 (over y, core), src: 8 (over z, x).
Axes of the slice: x: 2, y: 2, z: 4, core: 2. Of those that a mesh axis runs over, the one named last changes fastest.
Arguments:
- test_points: float32 [8, 3, 1024], P('test'), may hold values from 0 to 1
- test_basis: bfloat16 [8, 1024, 384], P('test'), may hold values from -0.1875 to 0.1875
- test_counts: int32 [8], P('test'), may hold values from 128 to 384, as said below
- source_points: float32 [64, 3, 1024], P('src'), may hold values from 0 to 1
- source_basis: bfloat16 [64, 1024, 384], P('src', 'test'), may hold values from -0.1875 to 0.1875
- source_counts: int32 [64], P('src'), may hold values from 128 to 384, as said below
- coefficients: bfloat16 [64, 384, 512], P('src'), may hold values from -0.0546875 to 0.0546875
Outputs:
- reduced: bfloat16 [8, 384, 64, 384], P('test', 'src')
- projected: bfloat16 [8, 384, 512], P('test', 'src')
Inputs may be any that keep to these rules, and one draw needn't show every extreme that they name: `test_counts`: number of leading basis columns of a test block that are used; the rest are ignored. Some test block uses all 384 in every draw. `source_counts`: number of leading basis columns of a source block that are used; the rest are ignored. Some source block uses all 384 in every draw.
All inputs are finite; a program needn't handle non-finite values.
Results may differ from a plain program's by a relative error of at most 0.015.
Values may be sent and summed in bfloat16 or wider, within the bound.
No kernel may reach another device: no remote copies, remote signals or barrier semaphores. Data moves between devices by JAX's collectives and lax.ppermute only.
A program may use at most 128 MiB of HBM per device.

v0:
```python
import functools

import jax
import jax.numpy as jnp
from jax import lax
from jax.experimental import pallas as pl
from jax.experimental.pallas import tpu as pltpu
from jax.sharding import PartitionSpec as P

softening = 0.0025
QBLOCK = 512
LANES = 128
VMEM_LIMIT = 255 * 256 * 1024
SMALL_VMEM_LIMIT = 32 * 1024 * 1024


def exchange(x, axis, flip):
    size = lax.axis_size(axis)
    return lax.ppermute(x, axis, [(a, a ^ flip) for a in range(size)])


def bits_down(size):
    bit = size // 2
    while bit >= 1:
        yield bit
        bit //= 2


def sum_rows(total, axis):
    size = lax.axis_size(axis)
    me = lax.axis_index(axis)
    held, bit = total, 1
    while held.shape[0] > 4:
        pairs = held.reshape((held.shape[0] // 2, 2) + held.shape[1:])
        mine = (me // bit) % 2
        keep = lax.dynamic_index_in_dim(pairs, mine, 1, keepdims=False)
        give = lax.dynamic_index_in_dim(pairs, 1 - mine, 1, keepdims=False)
        got = exchange(give, axis, bit)
        held = (keep.astype(jnp.float32) + got.astype(jnp.float32)).astype(held.dtype)
        bit *= 2
    mine = me // bit
    parts = [lax.dynamic_index_in_dim(held, mine, 0, keepdims=False)]
    for flip in range(1, held.shape[0]):
        give = lax.dynamic_index_in_dim(held, mine ^ flip, 0, keepdims=False)
        parts.append(exchange(give, axis, flip * bit))
    return parts


def rank_blocks(counts, cut):
    ranks = []
    for j, mine in enumerate(counts):
        rank = jnp.int32(0)
        for k, other in enumerate(counts):
            if k != j:
                ahead = other >= mine if k < j else other > mine
                rank += ahead.astype(jnp.int32)
        ranks.append(rank)
    offsets = []
    for j in range(len(counts)):
        offset = jnp.int32(0)
        for k, other in enumerate(counts):
            if k != j:
                offset += jnp.where((ranks[k] >= cut) & (ranks[k] < ranks[j]), other, 0)
        offsets.append(offset)
    return ranks, offsets


def pick_kernel(cut, counts_ref, basis_ref, order_ref, offsets_ref, first_ref, rest_ref):
    nblock = basis_ref.shape[0]
    ranks, offsets = rank_blocks([counts_ref[j] for j in range(nblock)], cut)
    for j in range(nblock):
        order_ref[ranks[j]] = jnp.int32(j)
        offsets_ref[j] = offsets[j]
    for place in range(nblock):
        block = basis_ref[order_ref[place]]
        if place < cut:
            first_ref[place] = block
        else:
            rest_ref[place - cut] = block


def pick(cut, counts, basis):
    nblock = basis.shape[0]
    smem, vmem = pl.BlockSpec(memory_space=pltpu.SMEM), pl.BlockSpec(memory_space=pltpu.VMEM)
    return pl.pallas_call(
        functools.partial(pick_kernel, cut),
        out_shape=(
            jax.ShapeDtypeStruct((nblock,), jnp.int32),
            jax.ShapeDtypeStruct((nblock,), jnp.int32),
            jax.ShapeDtypeStruct((cut,) + basis.shape[1:], basis.dtype),
            jax.ShapeDtypeStruct((nblock - cut,) + basis.shape[1:], basis.dtype),
        ),
        in_specs=[smem, vmem],
        out_specs=(smem, smem, vmem, vmem),
        compiler_params=pltpu.CompilerParams(vmem_limit_bytes=VMEM_LIMIT),
    )(counts, basis)


def tables_kernel(cut, nblock, widths, me_ref, *refs):
    *group_refs, counts_ref, order_ref, offsets_ref, branch_ref, joined_ref = refs
    group, inner = group_refs[0].shape[0], len(group_refs)
    for place, group_ref in enumerate(group_refs):
        for k in range(group):
            joined_ref[place * group + k] = group_ref[k]

    def step(source, need):
        base = source * nblock
        offset = source ^ me_ref[0]
        theirs = (offset % inner) * group + (offset // inner) * nblock
        counts = [joined_ref[theirs + j] for j in range(nblock)]
        ranks, offsets = rank_blocks(counts, cut)
        used = jnp.int32(0)
        for j in range(nblock):
            counts_ref[base + j] = counts[j]
            order_ref[base + ranks[j]] = jnp.int32(j)
            offsets_ref[base + j] = offsets[j]
            used += jnp.where(ranks[j] >= cut, counts[j], 0)
        return jnp.maximum(need, used)

    need = lax.fori_loop(0, counts_ref.shape[0] // nblock, step, jnp.int32(0))
    branch = jnp.int32(0)
    for width in widths[:-1]:
        branch += (need > width).astype(jnp.int32)
    branch_ref[0] = branch


def all_tables(cut, nblock, widths, me, groups):
    smem = pl.BlockSpec(memory_space=pltpu.SMEM)
    total = sum(group.shape[0] for group in groups)
    table = jax.ShapeDtypeStruct((total,), jnp.int32)
    return pl.pallas_call(
        functools.partial(tables_kernel, cut, nblock, widths),
        out_shape=(table, table, table, jax.ShapeDtypeStruct((1,), jnp.int32)),
        in_specs=[smem] * (1 + len(groups)),
        out_specs=(smem,) * 4,
        scratch_shapes=[pltpu.SMEM((total,), jnp.int32)],
    )(me, *groups)


NFEATURE = 128


def fill_features(rows_ref, points, is_test):
    def three_terms(x):
        high = x.astype(jnp.bfloat16).astype(jnp.float32)
        middle = (x - high).astype(jnp.bfloat16).astype(jnp.float32)
        return high, middle, x - high - middle

    centred = points - 0.5
    norm = jnp.sum(centred * centred, axis=0, keepdims=True)
    terms = three_terms(centred)
    norms = three_terms(norm + softening if is_test else norm)
    for a in range(3):
        for b in range(3):
            place = 3 * (3 * a + b)
            rows_ref[place : place + 3, :] = -2.0 * terms[a] if is_test else terms[b]
    for a in range(3):
        rows_ref[27 + a : 28 + a, :] = norms[a] if is_test else jnp.ones_like(norm)
        rows_ref[30 + a : 31 + a, :] = jnp.ones_like(norm) if is_test else norms[a]


def left_kernel(
    nshard, first, me_ref, order_ref, test_ref, source_ref, basis_ref, out_ref,
    rows_ref, features_ref, turned_ref, near_ref,
):
    j = pl.program_id(0)
    ntest = test_ref.shape[1]
    nq = source_ref.shape[2]
    part = nq // nshard
    block = min(QBLOCK, nq)

    @pl.when(j == 0)
    def _():
        rows_ref[...] = jnp.zeros_like(rows_ref)
        for i in range(ntest):
            fill_features(rows_ref, test_ref[:, i, :], True)
            features_ref[i] = rows_ref[...].T.astype(jnp.bfloat16)
            turned_ref[i] = basis_ref[i].T

    source = order_ref[first + j]
    for comp in range(3):
        rows_ref[comp : comp + 1, :] = source_ref[comp, pl.ds(source, 1), :]
    pieces = []
    for offset in range(nshard):
        start = pl.multiple_of((me_ref[0] ^ offset) * part, part)
        pieces.append(rows_ref[0:3, pl.ds(start, part)])
    fill_features(rows_ref, jnp.concatenate(pieces, axis=1), False)
    near_ref[...] = rows_ref[...].astype(jnp.bfloat16)

    steps = [(i, start) for i in range(ntest) for start in range(0, nq, block)]

    def kernel_block(i, start):
        squared = jnp.dot(
            features_ref[i], near_ref[:, start : start + block], preferred_element_type=jnp.float32
        )
        return lax.rsqrt(squared.astype(jnp.bfloat16))

    ready = kernel_block(*steps[0])
    for place, (i, start) in enumerate(steps):
        now = ready
        if place + 1 < len(steps):
            ready = kernel_block(*steps[place + 1])
        out_ref[i, 0, :, start : start + block] = jnp.dot(
            turned_ref[i], now, preferred_element_type=jnp.float32
        ).astype(jnp.bfloat16)


def left_products(nshard, me, order, test_points, source_points, test_basis, first, last):
    _, ntest, npoint = test_points.shape
    nall, nq = source_points.shape[1:]
    kmax = test_basis.shape[2]
    nsource = last - first
    return pl.pallas_call(
        functools.partial(left_kernel, nshard, first),
        grid_spec=pltpu.PrefetchScalarGridSpec(
            num_scalar_prefetch=2,
            grid=(nsource,),
            in_specs=[
                pl.BlockSpec((3, ntest, npoint), lambda j, *_: (0, 0, 0)),
                pl.BlockSpec((3, nall, nq), lambda j, *_: (0, 0, 0)),
                pl.BlockSpec((ntest, npoint, kmax), lambda j, *_: (0, 0, 0)),
            ],
            out_specs=pl.BlockSpec((ntest, 1, kmax, nq), lambda j, *_: (0, j, 0, 0)),
            scratch_shapes=[
                pltpu.VMEM((NFEATURE, npoint), jnp.float32),
                pltpu.VMEM((ntest, npoint, NFEATURE), jnp.bfloat16),
                pltpu.VMEM((ntest, kmax, npoint), jnp.bfloat16),
                pltpu.VMEM((NFEATURE, nq), jnp.bfloat16),
            ],
        ),
        out_shape=jax.ShapeDtypeStruct((ntest, nsource, kmax, nq), jnp.bfloat16),
        compiler_params=pltpu.CompilerParams(vmem_limit_bytes=VMEM_LIMIT),
        cost_estimate=pl.CostEstimate(
            flops=2 * ntest * nsource * npoint * nq * kmax,
            bytes_accessed=2 * ntest * nsource * kmax * nq,
            transcendentals=ntest * nsource * npoint * nq,
        ),
    )(me, order, test_points, source_points, test_basis)


def tile_kernel(nshard, first, packed, *refs):
    order_ref, source_counts_ref, offsets_ref, test_counts_ref, left_ref = refs[:5]
    shard_refs = refs[5 : 5 + nshard]
    j = pl.program_id(0)
    if packed:
        tile_ref, main_ref, over_ref, pack_ref = refs[5 + nshard :]
    else:
        (tile_ref,) = refs[5 + nshard :]
    ntest, _, kmax, _ = left_ref.shape
    ndest, _, _, rows, width = tile_ref.shape
    count = source_counts_ref[order_ref[first + j]]

    def work(wide):
        side = jnp.concatenate([shard_ref[0, :, :wide] for shard_ref in shard_refs], axis=0)
        row_ids = lax.broadcasted_iota(jnp.int32, (kmax, wide), 0)
        column_ids = lax.broadcasted_iota(jnp.int32, (kmax, wide), 1)
        products = [
            jnp.dot(left_ref[i, 0], side, preferred_element_type=jnp.float32) for i in range(ntest)
        ]
        if packed:
            offset = offsets_ref[order_ref[first + j]]
            shift = offset % LANES
            base = offset - shift
            low = lax.broadcasted_iota(jnp.int32, (kmax, LANES), 1) < shift
        for i in range(ntest):
            used = (row_ids < test_counts_ref[i]) & (column_ids < count)
            tile = jnp.where(used, products[i], 0.0)
            for dest in range(ndest):
                tile_ref[dest, i, 0, :, :wide] = tile[dest * rows : (dest + 1) * rows].astype(jnp.bfloat16)
                if wide < width:
                    tile_ref[dest, i, 0, :, wide:] = jnp.zeros((rows, width - wide), jnp.bfloat16)
            if not packed:
                continue
            rolled = [
                pltpu.roll(tile[:, start : start + LANES], shift, axis=1) for start in range(0, wide, LANES)
            ]
            for place in range(len(rolled) + 1):
                here = pl.ds(pl.multiple_of(base + place * LANES, LANES), LANES)
                if place == 0:
                    before = jnp.concatenate(
                        [pack_ref[dest, i, :, here].astype(jnp.float32) for dest in range(ndest)], axis=0
                    )
                else:
                    before = rolled[place - 1]
                after = rolled[place] if place < len(rolled) else jnp.zeros_like(before)
                window = jnp.where(low, before, after)
                for dest in range(ndest):
                    pack_ref[dest, i, :, here] = window[dest * rows : (dest + 1) * rows].astype(jnp.bfloat16)

    narrow = width - LANES
    if narrow > 0:
        pl.when(count <= narrow)(lambda: work(narrow))
        pl.when(count > narrow)(lambda: work(width))
    else:
        work(width)

    if packed:

        @pl.when(j == pl.num_programs(0) - 1)
        def _():
            main = main_ref.shape[3]
            main_ref[...] = pack_ref[:, :, :, :main]
            over_ref[...] = pack_ref[:, :, :, main : main + over_ref.shape[3]]


def tiles(ndest, first, tables, test_counts, left, shards, main):
    ntest, nsource, kmax, nq = left.shape
    nshard = len(shards)
    part, width = shards[0].shape[1:]
    rows = kmax // ndest
    packed = main is not None
    shapes = [jax.ShapeDtypeStruct((ndest, ntest, nsource, rows, width), jnp.bfloat16)]
    specs = [pl.BlockSpec((ndest, ntest, 1, rows, width), lambda j, *_: (0, 0, j, 0, 0))]
    scratch = []
    if packed:
        for columns in (main, nsource * width - main):
            shape = (ndest, ntest, rows, columns)
            shapes.append(jax.ShapeDtypeStruct(shape, jnp.bfloat16))
            specs.append(pl.BlockSpec(shape, lambda j, *_: (0, 0, 0, 0)))
        scratch.append(pltpu.VMEM((ndest, ntest, rows, nsource * width + LANES), jnp.bfloat16))
    return pl.pallas_call(
        functools.partial(tile_kernel, nshard, first, packed),
        grid_spec=pltpu.PrefetchScalarGridSpec(
            num_scalar_prefetch=4,
            grid=(nsource,),
            in_specs=[pl.BlockSpec((ntest, 1, kmax, nq), lambda j, *_: (0, j, 0, 0))]
            + [pl.BlockSpec((1, part, width), lambda j, *_: (j, 0, 0))] * nshard,
            out_specs=specs,
            scratch_shapes=scratch,
        ),
        out_shape=shapes,
        compiler_params=pltpu.CompilerParams(vmem_limit_bytes=VMEM_LIMIT),
        cost_estimate=pl.CostEstimate(
            flops=2 * ntest * nsource * kmax * width * nq,
            bytes_accessed=2 * ntest * nsource * kmax * (nq + width),
            transcendentals=0,
        ),
    )(*tables, test_counts, left, *shards)


def project_kernel(started, order_ref, tile_ref, coeff_ref, *refs):
    if started:
        start_ref, sum_ref, total_ref = refs
    else:
        *counts_refs, sum_ref, joined_ref, total_ref = refs
    j = pl.program_id(0)
    ndest, ntest, _, rows, _ = tile_ref.shape
    whole = [tile_ref[dest, i, 0] for i in range(ntest) for dest in range(ndest)]
    term = jnp.dot(jnp.concatenate(whole, axis=0), coeff_ref[0], preferred_element_type=jnp.float32)

    @pl.when(j == 0)
    def _():
        total_ref[...] = term + start_ref[...] if started else term

    @pl.when(j > 0)
    def _():
        total_ref[...] += term

    @pl.when(j == pl.num_programs(0) - 1)
    def _():
        if not started:
            sum_ref[...] = total_ref[...]
            nblock = counts_refs[0].shape[0]
            for place, counts_ref in enumerate(counts_refs):
                for k in range(nblock):
                    joined_ref[place * nblock + k] = counts_ref[k]
            return
        for i in range(ntest):
            for dest in range(ndest):
                top = (i * ndest + dest) * rows
                sum_ref[dest, i] = total_ref[top : top + rows, :].astype(sum_ref.dtype)


def project(order, first, tiles, coefficients, start=None, counts=()):
    ndest, ntest, nsource, rows, width = tiles.shape
    ncol = coefficients.shape[2]
    smem = pl.BlockSpec(memory_space=pltpu.SMEM)
    total_spec = pl.BlockSpec((ntest * ndest * rows, ncol), lambda j, order: (0, 0))
    started = start is not None
    if started:
        more, more_specs = [start], [total_spec]
        out_specs = pl.BlockSpec((ndest, ntest, rows, ncol), lambda j, order: (0, 0, 0, 0))
        out_shape = jax.ShapeDtypeStruct((ndest, ntest, rows, ncol), jnp.bfloat16)
    else:
        more, more_specs = list(counts), [smem] * len(counts)
        out_specs = (total_spec, smem)
        out_shape = (
            jax.ShapeDtypeStruct((ntest * ndest * rows, ncol), jnp.float32),
            jax.ShapeDtypeStruct((sum(part.shape[0] for part in counts),), jnp.int32),
        )
    return pl.pallas_call(
        functools.partial(project_kernel, started),
        grid_spec=pltpu.PrefetchScalarGridSpec(
            num_scalar_prefetch=1,
            grid=(nsource,),
            in_specs=[
                pl.BlockSpec((ndest, ntest, 1, rows, width), lambda j, order: (0, 0, j, 0, 0)),
                pl.BlockSpec((1, width, ncol), lambda j, order: (order[first + j], 0, 0)),
            ]
            + more_specs,
            out_specs=out_specs,
            scratch_shapes=[pltpu.VMEM((ntest * ndest * rows, ncol), jnp.float32)],
        ),
        out_shape=out_shape,
        compiler_params=pltpu.CompilerParams(vmem_limit_bytes=VMEM_LIMIT),
        cost_estimate=pl.CostEstimate(
            flops=2 * ndest * ntest * rows * width * ncol * nsource,
            bytes_accessed=2 * ndest * ntest * rows * width * nsource,
            transcendentals=0,
        ),
    )(order, tiles, coefficients, *more)


def unpack_kernel(cut, order_ref, counts_ref, offsets_ref, whole_ref, packed_ref, *refs):
    *part_refs, out_ref, sum_ref, rows_ref = refs
    sum_ref[...] = sum(part_ref[...].astype(jnp.float32) for part_ref in part_refs).astype(sum_ref.dtype)
    nsrc, _, _, rows, width = whole_ref.shape
    packed_width = packed_ref.shape[3]
    nall = out_ref.shape[2]
    nblock = nall // nsrc
    ntile = width // LANES
    step = 16 if rows % 16 == 0 else rows
    lanes = lax.broadcasted_iota(jnp.int32, (rows, LANES), 1)

    @pl.loop(0, nsrc, unroll=2)
    def _(source):
        for place in range(nblock):
            block = order_ref[source * nblock + place]
            target = source * nblock + block
            if place < cut:
                rows_ref[target] = whole_ref[source, 0, place].astype(jnp.float32)
                continue
            count = counts_ref[target]
            offset = offsets_ref[target]
            shift = offset % LANES
            base = offset - shift
            back = (LANES - shift) % LANES
            low = lanes < LANES - shift
            rolled = []
            for tile in range(ntile + 1):
                start = pl.multiple_of(jnp.minimum(base + tile * LANES, packed_width - LANES), LANES)
                piece = packed_ref[source, 0, :, pl.ds(start, LANES)].astype(jnp.float32)
                rolled.append(pltpu.roll(piece, back, axis=1))
            for tile in range(ntile):
                value = jnp.where(low, rolled[tile], rolled[tile + 1])
                value = jnp.where(lanes < count - tile * LANES, value, 0.0)
                rows_ref[target, :, tile * LANES : (tile + 1) * LANES] = value

    @pl.loop(0, nall // 16)
    def _(group):
        here = pl.ds(pl.multiple_of(group * 16, 16), 16)
        for top in range(0, rows, step):
            turned = jnp.transpose(rows_ref[here, top : top + step, :], (1, 0, 2))
            out_ref[0, top : top + step, here, :] = turned.astype(out_ref.dtype)


def unpack(cut, tables, whole, packed, parts):
    nsrc, ntest, _, rows, width = whole.shape
    packed_width = packed.shape[3]
    nall = tables[0].shape[0]
    sum_spec = pl.BlockSpec((1,) + parts[0].shape[1:], lambda i, *_: (i, 0, 0))
    return pl.pallas_call(
        functools.partial(unpack_kernel, cut),
        grid_spec=pltpu.PrefetchScalarGridSpec(
            num_scalar_prefetch=3,
            grid=(ntest,),
            in_specs=[
                pl.BlockSpec((nsrc, 1, cut, rows, width), lambda i, *_: (0, i, 0, 0, 0)),
                pl.BlockSpec((nsrc, 1, rows, packed_width), lambda i, *_: (0, i, 0, 0)),
            ]
            + [sum_spec] * len(parts),
            out_specs=(pl.BlockSpec((1, rows, nall, width), lambda i, *_: (i, 0, 0, 0)), sum_spec),
            scratch_shapes=[pltpu.VMEM((nall, rows, width), jnp.float32)],
        ),
        out_shape=(
            jax.ShapeDtypeStruct((ntest, rows, nall, width), jnp.bfloat16),
            jax.ShapeDtypeStruct(parts[0].shape, jnp.bfloat16),
        ),
        compiler_params=pltpu.CompilerParams(vmem_limit_bytes=SMALL_VMEM_LIMIT),
    )(*tables, whole, packed, *parts)


def body(
    test_points, test_basis, test_counts, source_points, source_basis, source_counts, coefficients
):
    nsource, part, kmax = source_basis.shape
    ntest = test_points.shape[0]
    nsrc = lax.axis_size("src")
    ntest_axis = lax.axis_size("test")
    me_test = lax.axis_index("test")
    cut = max(1, nsource * 3 // 8)

    held = {}

    def gather(name, shard, left):
        got = {0: shard}
        bits = list(bits_down(ntest_axis))
        for bit in bits:
            if bit == bits[-1]:
                names = [o for o in got if o != 0]
                tied = lax.optimization_barrier(tuple(got[o] for o in names) + (left,))
                got.update(zip(names, tied[:-1]))
                left = tied[-1]
            for offset in list(got):
                got[offset ^ bit] = exchange(got[offset], "test", bit)
            if bit == bits[0]:
                held[name] = got[bit]
        return [got[offset] for offset in sorted(got)], left

    most = (nsource - cut) * kmax
    main = min(most, -(-most * 18 // (25 * LANES)) * LANES)
    widths = [main, min(most, main + LANES), min(most, main + 2 * LANES), most]

    order, offsets, basis_a, basis_b = pick(cut, source_counts, source_basis)
    tables = (order, source_counts, offsets)
    me = jnp.reshape(me_test, (1,))
    test_points, source_points = test_points.transpose(1, 0, 2), source_points.transpose(1, 0, 2)

    left_a = left_products(ntest_axis, me, order, test_points, source_points, test_basis, 0, cut)
    shards_a, left_a = gather("a", basis_a, left_a)
    (tiles_a,) = tiles(nsrc, 0, tables, test_counts, left_a, shards_a, None)
    moved_a = lax.all_to_all(tiles_a, "src", split_axis=0, concat_axis=0, tiled=True)

    rest, _ = lax.optimization_barrier((basis_b, held["a"]))
    later, _ = lax.optimization_barrier((source_points, tiles_a))
    left_b = left_products(ntest_axis, me, order, test_points, later, test_basis, cut, nsource)
    shards_b, left_b = gather("b", rest, left_b)
    inner = max(1, nsrc // 4)
    counts, _ = lax.optimization_barrier((source_counts, left_b))
    far = [exchange(counts, "src", flip) for flip in range(inner, nsrc, inner)]
    tiles_b, packed, beyond = tiles(nsrc, cut, tables, test_counts, left_b, shards_b, main)
    packed, *far = lax.optimization_barrier((packed, *far))
    moved_b = lax.all_to_all(packed, "src", split_axis=0, concat_axis=0, tiled=True)

    sums, joined = project(order, 0, tiles_a, coefficients, counts=[source_counts] + far)
    groups = [joined] + [exchange(joined, "src", flip) for flip in range(1, inner)]
    sums = project(order, cut, tiles_b, coefficients, sums)
    parts = sum_rows(sums, "src")
    me_src, _ = lax.optimization_barrier((jnp.reshape(lax.axis_index("src"), (1,)), packed))
    all_counts, all_order, all_offsets, branch = all_tables(cut, nsource, widths, me_src, groups)
    spread = (all_order, all_counts, all_offsets)

    def finish(width, beyond, moved_a, moved_b, spread, parts):
        if width > main:
            more = lax.all_to_all(
                beyond[..., : width - main], "src", split_axis=0, concat_axis=0, tiled=True
            )
            moved_b = jnp.concatenate([moved_b, more], axis=3)
        return unpack(cut, spread, moved_a, moved_b, parts)

    return lax.switch(
        branch[0],
        [functools.partial(finish, width) for width in widths],
        beyond,
        moved_a,
        moved_b,
        spread,
        parts,
    )


def solution(mesh):
    return jax.shard_map(
        body,
        mesh=mesh,
        in_specs=(
            P("test", None, None),
            P("test", None, None),
            P("test"),
            P("src", None, None),
            P("src", "test", None),
            P("src"),
            P("src", None, None),
        ),
        out_specs=(P("test", "src", None, None), P("test", "src", None)),
        check_vma=False,
    )
```

profile of v0, /device:TPU:0, one launch (start us, length us, event | category | flops | bytes accessed | tf_op | source)
XLA Modules:
  0.0 145.7 jit_solution(18045360290001209330)
XLA Ops:
  0.6 2.8 %shard_map.94 = (s32[8]{0:T(128)}, s32[8]{0:T(128)}, bf16[3,256,384]{2,1,0:T(8,128)(2,1)}, bf16[5,256,384]{2,1,0:T(8,128)(2,1)}) custom-call(s32[8]{0:T(128)} %refs_0_.1, bf16[8,256,384]{2,1,0:T(8,128)(2,1)} %basis_ref.3), custom_call_target="tpu_custom_call" | custom-call | tf_op jit(solution)/shard_map/pallas_call | solution.py:85
  3.4 3.0 %collective-permute-start = (bf16[3,256,384]{2,1,0:T(8,128)(2,1)}, bf16[3,256,384]{2,1,0:T(8,128)(2,1)}, u32[]{:S(2)}, u32[]{:S(2)}) collective-permute-start(bf16[3,256,384]{2,1,0:T(8,128)(2,1)} %get-tuple-element.147.refs_5_), channel_id=1, source_target_pairs={{0,16},{8,24},{16,0},{24,8},{1,17},{9,25},{17,1},{25,9},{2,18},{10... | collective-permute-start | bytes 1769480 | tf_op jit(solution)/shard_map/ppermute | solution.py:19
  6.5 0.0 collective-permute-start.2
  6.5 14.0 %shard_map.95.refs_4_ = bf16[2,3,384,1024]{3,2,1,0:T(8,128)(2,1)} custom-call(s32[1]{0:T(128)} %bitcast.1.me_ref, s32[8]{0:T(128)} %get-tuple-element.144.order_ref.refs_0_, f32[3,2,1024]{2,1,0:T(2,128)} %bitcast.23, f32[3,8,1024]{2,1,0:T(8,128)} %bitcast.21, bf16[2,1024,384]{2,1,0:T(8,128)(2,1)} %basis_ref.5), custom_call_target="tpu_custom_call" | custom-call | flops 4831838208 | bytes 4718592 | tf_op jit(solution)/shard_map/pallas_call | solution.py:213
  20.5 0.0 collective-permute-done.refs_7_
  20.5 0.5 collective-permute-start.3
  21.0 0.0 collective-permute-done.2.refs_6_
  21.0 2.0 %collective-permute-done.3.refs_8_ = bf16[3,256,384]{2,1,0:T(8,128)(2,1)} collective-permute-done((bf16[3,256,384]{2,1,0:T(8,128)(2,1)}, bf16[3,256,384]{2,1,0:T(8,128)(2,1)}, u32[]{:S(2)}, u32[]{:S(2)}) %collective-permute-start.3) | collective-permute-done | bytes 589856 | tf_op jit(solution)/shard_map/ppermute | solution.py:19
  23.0 6.9 %shard_map.96.tile_ref = bf16[8,2,3,48,384]{4,3,2,1,0:T(8,128)(2,1)} custom-call(s32[8]{0:T(128)} %get-tuple-element.144.order_ref.refs_0_, s32[8]{0:T(128)} %refs_0_.1, s32[8]{0:T(128)} %get-tuple-element.145.refs_2_, s32[2]{0:T(128)} %refs_3_.3, bf16[2,3,384,1024]{3,2,1,0:T(8,128)(2,1)} %shard_map.95.refs_4_, ...), custom_call_target="tpu_custom_call" | custom-call | flops 1811939328 | bytes 6488064 | tf_op jit(solution)/shard_map/pallas_call | solution.py:321
  29.9 5.4 %all-to-all-start.3 = ((bf16[8,2,3,48,384]{4,3,2,1,0:T(8,128)(2,1)}), bf16[8,2,3,48,384]{4,3,2,1,0:T(8,128)(2,1)}, u32[]{:S(2)}, u32[]{:S(2)}) async-start(bf16[8,2,3,48,384]{4,3,2,1,0:T(8,128)(2,1)} %shard_map.96.tile_ref), calls=%async_computation.3 | async-start | bytes 3538944 | tf_op jit(solution)/shard_map/all_to_all | solution.py:522
  35.3 1.3 collective-permute-start.1
  36.6 0.0 collective-permute-start.4
  36.6 20.6 %shard_map.97.refs_4_ = bf16[2,5,384,1024]{3,2,1,0:T(8,128)(2,1)} custom-call(s32[1]{0:T(128)} %bitcast.1.me_ref, s32[8]{0:T(128)} %get-tuple-element.144.order_ref.refs_0_, f32[3,2,1024]{2,1,0:T(2,128)} %bitcast.24, f32[3,8,1024]{2,1,0:T(8,128)} %bitcast.22, bf16[2,1024,384]{2,1,0:T(8,128)(2,1)} %basis_ref.5), custom_call_target="tpu_custom_call" | custom-call | flops 8053063680 | bytes 7864320 | tf_op jit(solution)/shard_map/pallas_call | solution.py:213
  57.2 2.2 %collective-permute-done.1.refs_7_ = bf16[5,256,384]{2,1,0:T(8,128)(2,1)} collective-permute-done((bf16[5,256,384]{2,1,0:T(8,128)(2,1)}, bf16[5,256,384]{2,1,0:T(8,128)(2,1)}, u32[]{:S(2)}, u32[]{:S(2)}) %collective-permute-start.1) | collective-permute-done | bytes 983072 | tf_op jit(solution)/shard_map/ppermute | solution.py:19
  59.4 0.0 collective-permute-start.5
  59.4 0.0 copy-done
  59.4 1.7 %collective-permute-start.6 = (s32[8]{0:T(128)S(1)}, s32[8]{0:T(128)S(1)}, u32[]{:S(2)}, u32[]{:S(2)}) collective-permute-start(s32[8]{0:T(128)S(1)} %copy-done), channel_id=1, source_target_pairs={{0,2},{1,3},{2,0},{3,1},{4,6},{5,7},{6,4},{7,5},{8,10},{9,11},{10,... | collective-permute-start | bytes 104 | tf_op jit(solution)/shard_map/ppermute | solution.py:19
  61.1 2.4 %collective-permute-start.7 = (s32[8]{0:T(128)S(1)}, s32[8]{0:T(128)S(1)}, u32[]{:S(2)}, u32[]{:S(2)}) collective-permute-start(s32[8]{0:T(128)S(1)} %copy-done), channel_id=1, source_target_pairs={{0,4},{1,5},{2,6},{3,7},{4,0},{5,1},{6,2},{7,3},{8,12},{9,13},{10,... | collective-permute-start | bytes 104 | tf_op jit(solution)/shard_map/ppermute | solution.py:19
  63.5 0.3 collective-permute-start.8
  63.8 0.0 collective-permute-done.4.refs_6_
  63.8 0.0 collective-permute-done.5.refs_8_
  63.8 11.0 %shard_map.98 = (bf16[8,2,5,48,384]{4,3,2,1,0:T(8,128)(2,1)}, bf16[8,2,48,1408]{3,2,1,0:T(8,128)(2,1)}, bf16[8,2,48,512]{3,2,1,0:T(8,128)(2,1)}) custom-call(s32[8]{0:T(128)} %get-tuple-element.144.order_ref.refs_0_, s32[8]{0:T(128)} %refs_0_.1, s32[8]{0:T(128)} %get-tuple-element.145.refs_2_, s32[2]{0:T(128)} %refs_3_.3, ...), custom_call_target="tpu_custom_call" | custom-call | flops 3019898880 | bytes 10813440 | tf_op jit(solution)/shard_map/pallas_call | solution.py:321
  74.8 0.0 collective-permute-done.6.refs_1_
  74.8 0.0 copy-start.1
  74.8 2.3 %collective-permute-done.7.refs_2_ = s32[8]{0:T(128)S(1)} collective-permute-done((s32[8]{0:T(128)S(1)}, s32[8]{0:T(128)S(1)}, u32[]{:S(2)}, u32[]{:S(2)}) %collective-permute-start.7) | collective-permute-done | bytes 64 | tf_op jit(solution)/shard_map/ppermute | solution.py:19
  77.2 0.0 collective-permute-done.8.refs_3_
  77.2 0.0 all-to-all-done.3
  77.2 4.5 %all-to-all-start.4 = ((bf16[8,2,48,1408]{3,2,1,0:T(8,128)(2,1)}), bf16[8,2,48,1408]{3,2,1,0:T(8,128)(2,1)}, u32[]{:S(2)}, u32[]{:S(2)}) async-start(bf16[8,2,48,1408]{3,2,1,0:T(8,128)(2,1)} %get-tuple-element.156), calls=%async_computation.4 | async-start | bytes 4325376 | tf_op jit(solution)/shard_map/all_to_all | solution.py:533
  81.7 0.0 copy-done.1
  81.8 5.7 %shard_map.99 = (f32[768,512]{1,0:T(8,128)}, s32[32]{0:T(128)}) custom-call(s32[8]{0:T(128)} %get-tuple-element.144.order_ref.refs_0_, bf16[8,2,3,48,384]{4,3,2,1,0:T(8,128)(2,1)} %shard_map.96.tile_ref, bf16[8,384,512]{2,1,0:T(8,128)(2,1)} %coeff_ref.3, s32[8]{0:T(128)} %refs_0_.1, s32[8]{0:T(128)} %copy-done.1, s32[8]{0:T(128)} %copy-done.2, s32[8]{0:T(128)} %copy-done.3), custom_call_target="tpu_custom_call" | custom-call | flops 905969664 | bytes 1769472 | tf_op jit(solution)/shard_map/pallas_call | solution.py:391
  87.5 7.9 %shard_map.101 = bf16[8,2,48,512]{3,2,1,0:T(8,128)(2,1)} custom-call(s32[8]{0:T(128)} %get-tuple-element.144.order_ref.refs_0_, bf16[8,2,5,48,384]{4,3,2,1,0:T(8,128)(2,1)} %get-tuple-element.166.tile_ref, bf16[8,384,512]{2,1,0:T(8,128)(2,1)} %coeff_ref.3, f32[768,512]{1,0:T(8,128)} %get-tuple-element.167.refs_0_), custom_call_target="tpu_custom_call" | custom-call | flops 1509949440 | bytes 2949120 | tf_op jit(solution)/shard_map/pallas_call | solution.py:391
  95.5 1.0 dynamic-slice_bitcast_fusion
  96.5 1.8 %collective-permute-start.10 = (bf16[4,2,48,512]{3,2,1,0:T(8,128)(2,1)S(1)}, bf16[4,2,48,512]{3,2,1,0:T(8,128)(2,1)S(1)}, u32[]{:S(2)}, u32[]{:S(2)}) collective-permute-start(bf16[4,2,48,512]{3,2,1,0:T(8,128)(2,1)S(1)} %dynamic-slice_bitcast_fusion), channel_id=1, source_target_pairs={{0,1},{1,0},{2,3},{3,2},{4,5},{5,4},{6,7},{7,6},{8,9},{9,8},{10,11... | collective-permute-start | bytes 1179656 | tf_op jit(solution)/shard_map/ppermute | solution.py:19
  98.3 18.8 %collective-permute-done.10 = bf16[4,2,48,512]{3,2,1,0:T(8,128)(2,1)S(1)} collective-permute-done((bf16[4,2,48,512]{3,2,1,0:T(8,128)(2,1)S(1)}, bf16[4,2,48,512]{3,2,1,0:T(8,128)(2,1)S(1)}, u32[]{:S(2)}, u32[]{:S(2)}) %collective-permute-start.10) | collective-permute-done | bytes 393248 | tf_op jit(solution)/shard_map/ppermute | solution.py:19
  117.1 1.1 fusion
  118.2 0.1 collective-permute-start.11
  118.3 6.8 %collective-permute-start.12 = (bf16[2,48,512]{2,1,0:T(8,128)(2,1)S(1)}, bf16[2,48,512]{2,1,0:T(8,128)(2,1)S(1)}, u32[]{:S(2)}, u32[]{:S(2)}) collective-permute-start(bf16[2,48,512]{2,1,0:T(8,128)(2,1)S(1)} %get-tuple-element.180), channel_id=1, source_target_pairs={{0,4},{1,5},{2,6},{3,7},{4,0},{5,1},{6,2},{7,3},{8,12},{9,13},{10,... | collective-permute-start | bytes 294920 | tf_op jit(solution)/shard_map/ppermute | solution.py:19
  125.1 0.0 collective-permute-start.13
  125.1 0.0 collective-permute-start.9
  125.1 3.5 %collective-permute-done.9.refs_1_ = s32[32]{0:T(128)S(1)} collective-permute-done((s32[32]{0:T(128)S(1)}, s32[32]{0:T(128)S(1)}, u32[]{:S(2)}, u32[]{:S(2)}) %collective-permute-start.9) | collective-permute-done | bytes 160 | tf_op jit(solution)/shard_map/ppermute | solution.py:19
  128.6 0.5 copy-done.5
  129.1 2.8 %shard_map.100 = (s32[64]{0:T(128)S(1)}, s32[64]{0:T(128)S(1)}, s32[64]{0:T(128)S(1)}, s32[1]{0:T(128)}) custom-call(s32[1]{0:T(128)} %bitcast.me_ref, s32[32]{0:T(128)} %get-tuple-element.161.refs_0_, s32[32]{0:T(128)} %copy-done.5), custom_call_target="tpu_custom_call" | custom-call | tf_op jit(solution)/shard_map/pallas_call | solution.py:131
  132.6 0.0 collective-permute-done.11
  132.6 5.5 %collective-permute-done.12 = bf16[2,48,512]{2,1,0:T(8,128)(2,1)S(1)} collective-permute-done((bf16[2,48,512]{2,1,0:T(8,128)(2,1)S(1)}, bf16[2,48,512]{2,1,0:T(8,128)(2,1)S(1)}, u32[]{:S(2)}, u32[]{:S(2)}) %collective-permute-start.12) | collective-permute-done | bytes 98336 | tf_op jit(solution)/shard_map/ppermute | solution.py:19
  138.2 0.0 collective-permute-done.13
  138.2 0.0 all-to-all-done.4
  138.2 7.5 %conditional.1 = ((bf16[2,48,64,384]{3,2,1,0:T(8,128)(2,1)}, bf16[2,48,512]{2,1,0:T(8,128)(2,1)})) conditional(s32[]{:T(128)} %bitcast.4, (s32[64]{0:T(128)S(1)}, s32[64]{0:T(128)S(1)}, s32[64]{0:T(128)S(1)}, bf16[8,2,3,48,384]{4,3,2,1,0:T(8,128)(2,1)}, bf16[8,2,48,1408]{3,2,1,0:T(8,128)(2,1)}, ...), branch_computations={%region_0.1_spmd, %region_1.2_spmd, %region_2.3_spmd, %region_3.4_... | conditional | flops 5898240 | bytes 7471112 | solution.py:551
  138.2 7.5 %branch_0_fun.1 = (bf16[2,48,64,384]{3,2,1,0:T(8,128)(2,1)}, bf16[2,48,512]{2,1,0:T(8,128)(2,1)}) custom-call(s32[64]{0:T(128)S(1)} %get-tuple-element.78.order_ref, s32[64]{0:T(128)S(1)} %get-tuple-element.79.counts_ref, s32[64]{0:T(128)S(1)} %get-tuple-element.80.offsets_ref, bf16[8,2,3,48,384]{4,3,2,1,0:T(8,128)(2,1)} %get-tuple-element.81.whole_ref, ...), custom_call_target="tpu_custom_call" | custom-call | tf_op jit(solution)/shard_map/cond/branch_0_fun/pallas_call | solution.py:462
  (9 shorter events, 0.1 us)
Async XLA Ops:
  3.4 17.0 %collective-permute-start = (bf16[3,256,384]{2,1,0:T(8,128)(2,1)}, bf16[3,256,384]{2,1,0:T(8,128)(2,1)}, u32[]{:S(2)}, u32[]{:S(2)}) collective-permute-start(bf16[3,256,384]{2,1,0:T(8,128)(2,1)} %get-tuple-element.147.refs_5_), channel_id=1, source_target_pairs={{0,16},{8,24},{16,0},{24,8},{1,17},{9,25},{17,1},{25,9},{2,18},{10... | collective-permute-start | bytes 1769480 | tf_op jit(solution)/shard_map/ppermute | solution.py:19
  6.5 14.5 %collective-permute-start.2 = (bf16[3,256,384]{2,1,0:T(8,128)(2,1)}, bf16[3,256,384]{2,1,0:T(8,128)(2,1)}, u32[]{:S(2)}, u32[]{:S(2)}) collective-permute-start(bf16[3,256,384]{2,1,0:T(8,128)(2,1)} %get-tuple-element.147.refs_5_), channel_id=1, source_target_pairs={{0,8},{8,0},{16,24},{24,16},{1,9},{9,1},{17,25},{25,17},{2,10},{10... | collective-permute-start | bytes 1769480 | tf_op jit(solution)/shard_map/ppermute | solution.py:19
  20.5 2.5 %collective-permute-start.3 = (bf16[3,256,384]{2,1,0:T(8,128)(2,1)}, bf16[3,256,384]{2,1,0:T(8,128)(2,1)}, u32[]{:S(2)}, u32[]{:S(2)}) collective-permute-start(bf16[3,256,384]{2,1,0:T(8,128)(2,1)} %collective-permute-done.refs_7_), channel_id=1, source_target_pairs={{0,8},{8,0},{16,24},{24,16},{1,9},{9,1},{17,25},{25,17},{2,10},{10... | collective-permute-start | bytes 1769480 | tf_op jit(solution)/shard_map/ppermute | solution.py:19
  29.9 47.3 %all-to-all-start.3 = ((bf16[8,2,3,48,384]{4,3,2,1,0:T(8,128)(2,1)}), bf16[8,2,3,48,384]{4,3,2,1,0:T(8,128)(2,1)}, u32[]{:S(2)}, u32[]{:S(2)}) async-start(bf16[8,2,3,48,384]{4,3,2,1,0:T(8,128)(2,1)} %shard_map.96.tile_ref), calls=%async_computation.3 | async-start | bytes 3538944 | tf_op jit(solution)/shard_map/all_to_all | solution.py:522
  35.3 24.1 %copy-start = (s32[8]{0:T(128)S(1)}, s32[8]{0:T(128)}, u32[]{:S(2)}) copy-start(s32[8]{0:T(128)} %refs_0_.1) | copy-start | bytes 100
  35.3 24.1 %collective-permute-start.1 = (bf16[5,256,384]{2,1,0:T(8,128)(2,1)}, bf16[5,256,384]{2,1,0:T(8,128)(2,1)}, u32[]{:S(2)}, u32[]{:S(2)}) collective-permute-start(bf16[5,256,384]{2,1,0:T(8,128)(2,1)} %get-tuple-element.148.refs_5_), channel_id=1, source_target_pairs={{0,16},{8,24},{16,0},{24,8},{1,17},{9,25},{17,1},{25,9},{2,18},{10... | collective-permute-start | bytes 2949128 | tf_op jit(solution)/shard_map/ppermute | solution.py:19
  36.6 27.2 %collective-permute-start.4 = (bf16[5,256,384]{2,1,0:T(8,128)(2,1)}, bf16[5,256,384]{2,1,0:T(8,128)(2,1)}, u32[]{:S(2)}, u32[]{:S(2)}) collective-permute-start(bf16[5,256,384]{2,1,0:T(8,128)(2,1)} %get-tuple-element.148.refs_5_), channel_id=1, source_target_pairs={{0,8},{8,0},{16,24},{24,16},{1,9},{9,1},{17,25},{25,17},{2,10},{10... | collective-permute-start | bytes 2949128 | tf_op jit(solution)/shard_map/ppermute | solution.py:19
  59.4 4.4 %collective-permute-start.5 = (bf16[5,256,384]{2,1,0:T(8,128)(2,1)}, bf16[5,256,384]{2,1,0:T(8,128)(2,1)}, u32[]{:S(2)}, u32[]{:S(2)}) collective-permute-start(bf16[5,256,384]{2,1,0:T(8,128)(2,1)} %collective-permute-done.1.refs_7_), channel_id=1, source_target_pairs={{0,8},{8,0},{16,24},{24,16},{1,9},{9,1},{17,25},{25,17},{2,10},{10... | collective-permute-start | bytes 2949128 | tf_op jit(solution)/shard_map/ppermute | solution.py:19
  59.4 15.4 %collective-permute-start.6 = (s32[8]{0:T(128)S(1)}, s32[8]{0:T(128)S(1)}, u32[]{:S(2)}, u32[]{:S(2)}) collective-permute-start(s32[8]{0:T(128)S(1)} %copy-done), channel_id=1, source_target_pairs={{0,2},{1,3},{2,0},{3,1},{4,6},{5,7},{6,4},{7,5},{8,10},{9,11},{10,... | collective-permute-start | bytes 104 | tf_op jit(solution)/shard_map/ppermute | solution.py:19
  61.1 16.1 %collective-permute-start.7 = (s32[8]{0:T(128)S(1)}, s32[8]{0:T(128)S(1)}, u32[]{:S(2)}, u32[]{:S(2)}) collective-permute-start(s32[8]{0:T(128)S(1)} %copy-done), channel_id=1, source_target_pairs={{0,4},{1,5},{2,6},{3,7},{4,0},{5,1},{6,2},{7,3},{8,12},{9,13},{10,... | collective-permute-start | bytes 104 | tf_op jit(solution)/shard_map/ppermute | solution.py:19
  63.5 13.7 %collective-permute-start.8 = (s32[8]{0:T(128)S(1)}, s32[8]{0:T(128)S(1)}, u32[]{:S(2)}, u32[]{:S(2)}) collective-permute-start(s32[8]{0:T(128)S(1)} %copy-done), channel_id=1, source_target_pairs={{0,6},{1,7},{2,4},{3,5},{4,2},{5,3},{6,0},{7,1},{8,14},{9,15},{10,... | collective-permute-start | bytes 104 | tf_op jit(solution)/shard_map/ppermute | solution.py:19
  74.8 6.9 %copy-start.1 = (s32[8]{0:T(128)}, s32[8]{0:T(128)S(1)}, u32[]{:S(2)}) copy-start(s32[8]{0:T(128)S(1)} %collective-permute-done.6.refs_1_) | copy-start | bytes 100
  77.2 4.6 %copy-start.2 = (s32[8]{0:T(128)}, s32[8]{0:T(128)S(1)}, u32[]{:S(2)}) copy-start(s32[8]{0:T(128)S(1)} %collective-permute-done.7.refs_2_) | copy-start | bytes 100
  77.2 4.6 %copy-start.3 = (s32[8]{0:T(128)}, s32[8]{0:T(128)S(1)}, u32[]{:S(2)}) copy-start(s32[8]{0:T(128)S(1)} %collective-permute-done.8.refs_3_) | copy-start | bytes 100
  77.2 61.0 %all-to-all-start.4 = ((bf16[8,2,48,1408]{3,2,1,0:T(8,128)(2,1)}), bf16[8,2,48,1408]{3,2,1,0:T(8,128)(2,1)}, u32[]{:S(2)}, u32[]{:S(2)}) async-start(bf16[8,2,48,1408]{3,2,1,0:T(8,128)(2,1)} %get-tuple-element.156), calls=%async_computation.4 | async-start | bytes 4325376 | tf_op jit(solution)/shard_map/all_to_all | solution.py:533
  87.5 37.6 %copy-start.4 = (s32[32]{0:T(128)S(1)}, s32[32]{0:T(128)}, u32[]{:S(2)}) copy-start(s32[32]{0:T(128)} %get-tuple-element.161.refs_0_) | copy-start | bytes 388
  96.5 20.6 %collective-permute-start.10 = (bf16[4,2,48,512]{3,2,1,0:T(8,128)(2,1)S(1)}, bf16[4,2,48,512]{3,2,1,0:T(8,128)(2,1)S(1)}, u32[]{:S(2)}, u32[]{:S(2)}) collective-permute-start(bf16[4,2,48,512]{3,2,1,0:T(8,128)(2,1)S(1)} %dynamic-slice_bitcast_fusion), channel_id=1, source_target_pairs={{0,1},{1,0},{2,3},{3,2},{4,5},{5,4},{6,7},{7,6},{8,9},{9,8},{10,11... | collective-permute-start | bytes 1179656 | tf_op jit(solution)/shard_map/ppermute | solution.py:19
  118.2 14.4 %collective-permute-start.11 = (bf16[2,48,512]{2,1,0:T(8,128)(2,1)S(1)}, bf16[2,48,512]{2,1,0:T(8,128)(2,1)S(1)}, u32[]{:S(2)}, u32[]{:S(2)}) collective-permute-start(bf16[2,48,512]{2,1,0:T(8,128)(2,1)S(1)} %get-tuple-element.181), channel_id=1, source_target_pairs={{0,2},{1,3},{2,0},{3,1},{4,6},{5,7},{6,4},{7,5},{8,10},{9,11},{10,... | collective-permute-start | bytes 294920 | tf_op jit(solution)/shard_map/ppermute | solution.py:19
  118.3 19.9 %collective-permute-start.12 = (bf16[2,48,512]{2,1,0:T(8,128)(2,1)S(1)}, bf16[2,48,512]{2,1,0:T(8,128)(2,1)S(1)}, u32[]{:S(2)}, u32[]{:S(2)}) collective-permute-start(bf16[2,48,512]{2,1,0:T(8,128)(2,1)S(1)} %get-tuple-element.180), channel_id=1, source_target_pairs={{0,4},{1,5},{2,6},{3,7},{4,0},{5,1},{6,2},{7,3},{8,12},{9,13},{10,... | collective-permute-start | bytes 294920 | tf_op jit(solution)/shard_map/ppermute | solution.py:19
  125.1 13.1 %collective-permute-start.13 = (bf16[2,48,512]{2,1,0:T(8,128)(2,1)S(1)}, bf16[2,48,512]{2,1,0:T(8,128)(2,1)S(1)}, u32[]{:S(2)}, u32[]{:S(2)}) collective-permute-start(bf16[2,48,512]{2,1,0:T(8,128)(2,1)S(1)} %get-tuple-element.179), channel_id=1, source_target_pairs={{0,6},{1,7},{2,4},{3,5},{4,2},{5,3},{6,0},{7,1},{8,14},{9,15},{10,... | collective-permute-start | bytes 294920 | tf_op jit(solution)/shard_map/ppermute | solution.py:19
  125.1 3.5 %collective-permute-start.9 = (s32[32]{0:T(128)S(1)}, s32[32]{0:T(128)S(1)}, u32[]{:S(2)}, u32[]{:S(2)}) collective-permute-start(s32[32]{0:T(128)S(1)} %copy-done.4), channel_id=1, source_target_pairs={{0,1},{1,0},{2,3},{3,2},{4,5},{5,4},{6,7},{7,6},{8,9},{9,8},{10,11... | collective-permute-start | bytes 392 | tf_op jit(solution)/shard_map/ppermute | solution.py:19
  128.6 0.5 copy-start.5
where the time goes:
time: 147 us; the launch traced here: 146 us
  Pallas kernels  79.3 us (54%)
  waiting for transfers between devices  34.4 us (23%)
  starting transfers between devices  27.8 us (19%)
  local copies, waits for them, and re-layouts  1.59 us (1%)
  between operations  1.48 us (1%)
    pallas_call x2, Pallas kernels, left_products(): pl.pallas_call(functools.partial(left_kernel, nshard, first), grid_spec=p...  34.6 us
    ppermute x14, waiting for transfers between devices, exchange(): return lax.ppermute(x, axis, [(a, a ^ flip) for a in range(size)])  34.4 us
    pallas_call x2, Pallas kernels, tiles(): pl.pallas_call(functools.partial(tile_kernel, nshard, first, packed), gri...  17.9 us
    ppermute x14, starting transfers between devices, exchange(): return lax.ppermute(x, axis, [(a, a ^ flip) for a in range(size)])  17.8 us
    pallas_call x2, Pallas kernels, project(): pl.pallas_call(functools.partial(project_kernel, started), grid_spec=pltp...  13.7 us
    pallas_call x1, Pallas kernels, unpack(): pl.pallas_call(functools.partial(unpack_kernel, cut), grid_spec=pltpu.Pre...  7.55 us
    all_to_all x1, starting transfers between devices, body(): lax.all_to_all(tiles_a, 'src', split_axis=0, concat_axis=0, tiled=True)  5.42 us
    all_to_all x1, starting transfers between devices, body(): lax.all_to_all(packed, 'src', split_axis=0, concat_axis=0, tiled=True)  4.54 us
  transfers between devices with their start and end apart: 16, of which 6 were waited for; matrix products, arithmetic and copies ran while one was open for 1% of the time, Pallas kernels for 43%

commit v1 on v0

--- a/solution.py
+++ b/solution.py
@@ -8,7 +8,7 @@
 from jax.sharding import PartitionSpec as P
 
 softening = 0.0025
-QBLOCK = 512
+QBLOCK = 256
 LANES = 128
 VMEM_LIMIT = 255 * 256 * 1024
 SMALL_VMEM_LIMIT = 32 * 1024 * 1024
@@ -30,7 +30,7 @@
     size = lax.axis_size(axis)
     me = lax.axis_index(axis)
     held, bit = total, 1
-    while held.shape[0] > 4:
+    while held.shape[0] > 2:
         pairs = held.reshape((held.shape[0] // 2, 2) + held.shape[1:])
         mine = (me // bit) % 2
         keep = lax.dynamic_index_in_dim(pairs, mine, 1, keepdims=False)

time: 147 us -> 151 us (1.027)
  waiting for transfers between devices: 34.4 us -> 43.9 us
  starting transfers between devices: 27.8 us -> 23.7 us
    ppermute x14 -> x13, waiting for transfers between devices: 34.4 us -> 43.9 us  [exchange(): return lax.ppermute(x, axis, [(a, a ^ flip) for a in range(size)])]
    ppermute x14 -> x13, starting transfers between devices: 17.8 us -> 13.6 us  [exchange(): return lax.ppermute(x, axis, [(a, a ^ flip) for a in range(size)])]
  transfers between devices with their start and end apart: 16 -> 15, of which waited for: 6 -> 7; matrix products, arithmetic and copies ran while one was open for 1% -> 2% of each run, Pallas kernels for 43% -> 40%
where the time goes in v1:
time: 151 us; the launch traced here: 150 us
  Pallas kernels  77.9 us (52%)
  waiting for transfers between devices  43.9 us (29%)
  starting transfers between devices  23.7 us (16%)
  local copies, waits for them, and re-layouts  1.67 us (1%)
  between operations  1.53 us (1%)
    ppermute x13, waiting for transfers between devices, exchange(): return lax.ppermute(x, axis, [(a, a ^ flip) for a in range(size)])  43.9 us
    pallas_call x2, Pallas kernels, left_products(): pl.pallas_call(functools.partial(left_kernel, nshard, first), grid_spec=p...  33.2 us
    pallas_call x2, Pallas kernels, tiles(): pl.pallas_call(functools.partial(tile_kernel, nshard, first, packed), gri...  17.9 us
    pallas_call x2, Pallas kernels, project(): pl.pallas_call(functools.partial(project_kernel, started), grid_spec=pltp...  13.7 us
    ppermute x13, starting transfers between devices, exchange(): return lax.ppermute(x, axis, [(a, a ^ flip) for a in range(size)])  13.6 us
    pallas_call x1, Pallas kernels, unpack(): pl.pallas_call(functools.partial(unpack_kernel, cut), grid_spec=pltpu.Pre...  7.53 us
    all_to_all x1, starting transfers between devices, body(): lax.all_to_all(tiles_a, 'src', split_axis=0, concat_axis=0, tiled=True)  5.63 us
    all_to_all x1, starting transfers between devices, body(): lax.all_to_all(packed, 'src', split_axis=0, concat_axis=0, tiled=True)  4.55 us
  transfers between devices with their start and end apart: 15, of which 7 were waited for; matrix products, arithmetic and copies ran while one was open for 2% of the time, Pallas kernels for 40%

profile of v1, /device:TPU:0, one launch (start us, length us, event | category | flops | bytes accessed | tf_op | source)
XLA Modules:
  0.0 149.9 jit_solution(10686499916645283117)
XLA Ops:
  0.6 2.8 %shard_map.94 = (s32[8]{0:T(128)}, s32[8]{0:T(128)}, bf16[3,256,384]{2,1,0:T(8,128)(2,1)}, bf16[5,256,384]{2,1,0:T(8,128)(2,1)}) custom-call(s32[8]{0:T(128)} %refs_0_.1, bf16[8,256,384]{2,1,0:T(8,128)(2,1)} %basis_ref.3), custom_call_target="tpu_custom_call" | custom-call | tf_op jit(solution)/shard_map/pallas_call | solution.py:85
  3.4 3.0 %collective-permute-start = (bf16[3,256,384]{2,1,0:T(8,128)(2,1)}, bf16[3,256,384]{2,1,0:T(8,128)(2,1)}, u32[]{:S(2)}, u32[]{:S(2)}) collective-permute-start(bf16[3,256,384]{2,1,0:T(8,128)(2,1)} %get-tuple-element.123.refs_5_), channel_id=1, source_target_pairs={{0,16},{8,24},{16,0},{24,8},{1,17},{9,25},{17,1},{25,9},{2,18},{10... | collective-permute-start | bytes 1769480 | tf_op jit(solution)/shard_map/ppermute | solution.py:19
  6.5 0.0 collective-permute-start.2
  6.5 13.5 %shard_map.95.refs_4_ = bf16[2,3,384,1024]{3,2,1,0:T(8,128)(2,1)} custom-call(s32[1]{0:T(128)} %bitcast.1.me_ref, s32[8]{0:T(128)} %get-tuple-element.120.order_ref.refs_0_, f32[3,2,1024]{2,1,0:T(2,128)} %bitcast.29, f32[3,8,1024]{2,1,0:T(8,128)} %bitcast.27, bf16[2,1024,384]{2,1,0:T(8,128)(2,1)} %basis_ref.5), custom_call_target="tpu_custom_call" | custom-call | flops 4831838208 | bytes 4718592 | tf_op jit(solution)/shard_map/pallas_call | solution.py:213
  19.9 0.2 collective-permute-done.refs_7_
  20.1 0.3 collective-permute-start.3
  20.4 0.0 collective-permute-done.2.refs_6_
  20.4 2.0 %collective-permute-done.3.refs_8_ = bf16[3,256,384]{2,1,0:T(8,128)(2,1)} collective-permute-done((bf16[3,256,384]{2,1,0:T(8,128)(2,1)}, bf16[3,256,384]{2,1,0:T(8,128)(2,1)}, u32[]{:S(2)}, u32[]{:S(2)}) %collective-permute-start.3) | collective-permute-done | bytes 589856 | tf_op jit(solution)/shard_map/ppermute | solution.py:19
  22.5 6.9 %shard_map.96.tile_ref = bf16[8,2,3,48,384]{4,3,2,1,0:T(8,128)(2,1)} custom-call(s32[8]{0:T(128)} %get-tuple-element.120.order_ref.refs_0_, s32[8]{0:T(128)} %refs_0_.1, s32[8]{0:T(128)} %get-tuple-element.121.refs_2_, s32[2]{0:T(128)} %refs_3_.3, bf16[2,3,384,1024]{3,2,1,0:T(8,128)(2,1)} %shard_map.95.refs_4_, ...), custom_call_target="tpu_custom_call" | custom-call | flops 1811939328 | bytes 6488064 | tf_op jit(solution)/shard_map/pallas_call | solution.py:321
  29.3 5.6 %all-to-all-start.3 = ((bf16[8,2,3,48,384]{4,3,2,1,0:T(8,128)(2,1)}), bf16[8,2,3,48,384]{4,3,2,1,0:T(8,128)(2,1)}, u32[]{:S(2)}, u32[]{:S(2)}) async-start(bf16[8,2,3,48,384]{4,3,2,1,0:T(8,128)(2,1)} %shard_map.96.tile_ref), calls=%async_computation.3 | async-start | bytes 3538944 | tf_op jit(solution)/shard_map/all_to_all | solution.py:522
  35.0 1.6 %collective-permute-start.1 = (bf16[5,256,384]{2,1,0:T(8,128)(2,1)}, bf16[5,256,384]{2,1,0:T(8,128)(2,1)}, u32[]{:S(2)}, u32[]{:S(2)}) collective-permute-start(bf16[5,256,384]{2,1,0:T(8,128)(2,1)} %get-tuple-element.124.refs_5_), channel_id=1, source_target_pairs={{0,16},{8,24},{16,0},{24,8},{1,17},{9,25},{17,1},{25,9},{2,18},{10... | collective-permute-start | bytes 2949128 | tf_op jit(solution)/shard_map/ppermute | solution.py:19
  36.6 0.0 collective-permute-start.4
  36.6 19.7 %shard_map.97.refs_4_ = bf16[2,5,384,1024]{3,2,1,0:T(8,128)(2,1)} custom-call(s32[1]{0:T(128)} %bitcast.1.me_ref, s32[8]{0:T(128)} %get-tuple-element.120.order_ref.refs_0_, f32[3,2,1024]{2,1,0:T(2,128)} %bitcast.30, f32[3,8,1024]{2,1,0:T(8,128)} %bitcast.28, bf16[2,1024,384]{2,1,0:T(8,128)(2,1)} %basis_ref.5), custom_call_target="tpu_custom_call" | custom-call | flops 8053063680 | bytes 7864320 | tf_op jit(solution)/shard_map/pallas_call | solution.py:213
  56.3 2.6 %collective-permute-done.1.refs_7_ = bf16[5,256,384]{2,1,0:T(8,128)(2,1)} collective-permute-done((bf16[5,256,384]{2,1,0:T(8,128)(2,1)}, bf16[5,256,384]{2,1,0:T(8,128)(2,1)}, u32[]{:S(2)}, u32[]{:S(2)}) %collective-permute-start.1) | collective-permute-done | bytes 983072 | tf_op jit(solution)/shard_map/ppermute | solution.py:19
  58.9 0.0 collective-permute-start.5
  58.9 0.0 copy-done.1
  58.9 1.7 %collective-permute-start.6 = (s32[8]{0:T(128)S(1)}, s32[8]{0:T(128)S(1)}, u32[]{:S(2)}, u32[]{:S(2)}) collective-permute-start(s32[8]{0:T(128)S(1)} %copy-done.1), channel_id=1, source_target_pairs={{0,2},{1,3},{2,0},{3,1},{4,6},{5,7},{6,4},{7,5},{8,10},{9,11},{10,... | collective-permute-start | bytes 104 | tf_op jit(solution)/shard_map/ppermute | solution.py:19
  60.6 2.4 %collective-permute-start.7 = (s32[8]{0:T(128)S(1)}, s32[8]{0:T(128)S(1)}, u32[]{:S(2)}, u32[]{:S(2)}) collective-permute-start(s32[8]{0:T(128)S(1)} %copy-done.1), channel_id=1, source_target_pairs={{0,4},{1,5},{2,6},{3,7},{4,0},{5,1},{6,2},{7,3},{8,12},{9,13},{10,... | collective-permute-start | bytes 104 | tf_op jit(solution)/shard_map/ppermute | solution.py:19
  62.9 0.3 collective-permute-start.8
  63.3 0.0 collective-permute-done.4.refs_6_
  63.3 0.0 collective-permute-done.5.refs_8_
  63.3 11.0 %shard_map.98 = (bf16[8,2,5,48,384]{4,3,2,1,0:T(8,128)(2,1)}, bf16[8,2,48,1408]{3,2,1,0:T(8,128)(2,1)}, bf16[8,2,48,512]{3,2,1,0:T(8,128)(2,1)}) custom-call(s32[8]{0:T(128)} %get-tuple-element.120.order_ref.refs_0_, s32[8]{0:T(128)} %refs_0_.1, s32[8]{0:T(128)} %get-tuple-element.121.refs_2_, s32[2]{0:T(128)} %refs_3_.3, ...), custom_call_target="tpu_custom_call" | custom-call | flops 3019898880 | bytes 10813440 | tf_op jit(solution)/shard_map/pallas_call | solution.py:321
  74.3 0.0 collective-permute-done.6.refs_1_
  74.3 0.0 copy-start.2
  74.3 2.4 %collective-permute-done.7.refs_2_ = s32[8]{0:T(128)S(1)} collective-permute-done((s32[8]{0:T(128)S(1)}, s32[8]{0:T(128)S(1)}, u32[]{:S(2)}, u32[]{:S(2)}) %collective-permute-start.7) | collective-permute-done | bytes 64 | tf_op jit(solution)/shard_map/ppermute | solution.py:19
  76.6 0.0 collective-permute-done.8.refs_3_
  76.6 0.0 all-to-all-done.3
  76.6 4.5 %all-to-all-start.4 = ((bf16[8,2,48,1408]{3,2,1,0:T(8,128)(2,1)}), bf16[8,2,48,1408]{3,2,1,0:T(8,128)(2,1)}, u32[]{:S(2)}, u32[]{:S(2)}) async-start(bf16[8,2,48,1408]{3,2,1,0:T(8,128)(2,1)} %get-tuple-element.132), calls=%async_computation.4 | async-start | bytes 4325376 | tf_op jit(solution)/shard_map/all_to_all | solution.py:533
  81.2 0.0 copy-done.2
  81.2 0.0 copy-done.3
  81.3 5.7 %shard_map.99 = (f32[768,512]{1,0:T(8,128)}, s32[32]{0:T(128)}) custom-call(s32[8]{0:T(128)} %get-tuple-element.120.order_ref.refs_0_, bf16[8,2,3,48,384]{4,3,2,1,0:T(8,128)(2,1)} %shard_map.96.tile_ref, bf16[8,384,512]{2,1,0:T(8,128)(2,1)} %coeff_ref.3, s32[8]{0:T(128)} %refs_0_.1, s32[8]{0:T(128)} %copy-done.2, s32[8]{0:T(128)} %copy-done.3, s32[8]{0:T(128)} %copy-done.4), custom_call_target="tpu_custom_call" | custom-call | flops 905969664 | bytes 1769472 | tf_op jit(solution)/shard_map/pallas_call | solution.py:391
  87.0 7.9 %shard_map.101 = bf16[8,2,48,512]{3,2,1,0:T(8,128)(2,1)} custom-call(s32[8]{0:T(128)} %get-tuple-element.120.order_ref.refs_0_, bf16[8,2,5,48,384]{4,3,2,1,0:T(8,128)(2,1)} %get-tuple-element.142.tile_ref, bf16[8,384,512]{2,1,0:T(8,128)(2,1)} %coeff_ref.3, f32[768,512]{1,0:T(8,128)} %get-tuple-element.143.refs_0_), custom_call_target="tpu_custom_call" | custom-call | flops 1509949440 | bytes 2949120 | tf_op jit(solution)/shard_map/pallas_call | solution.py:391
  94.9 1.1 dynamic-slice_bitcast_fusion
  96.0 1.7 %collective-permute-start.10 = (bf16[4,2,48,512]{3,2,1,0:T(8,128)(2,1)S(1)}, bf16[4,2,48,512]{3,2,1,0:T(8,128)(2,1)S(1)}, u32[]{:S(2)}, u32[]{:S(2)}) collective-permute-start(bf16[4,2,48,512]{3,2,1,0:T(8,128)(2,1)S(1)} %dynamic-slice_bitcast_fusion), channel_id=1, source_target_pairs={{0,1},{1,0},{2,3},{3,2},{4,5},{5,4},{6,7},{7,6},{8,9},{9,8},{10,11... | collective-permute-start | bytes 1179656 | tf_op jit(solution)/shard_map/ppermute | solution.py:19
  97.8 18.7 %collective-permute-done.10 = bf16[4,2,48,512]{3,2,1,0:T(8,128)(2,1)S(1)} collective-permute-done((bf16[4,2,48,512]{3,2,1,0:T(8,128)(2,1)S(1)}, bf16[4,2,48,512]{3,2,1,0:T(8,128)(2,1)S(1)}, u32[]{:S(2)}, u32[]{:S(2)}) %collective-permute-start.10) | collective-permute-done | bytes 393248 | tf_op jit(solution)/shard_map/ppermute | solution.py:19
  116.5 1.1 fusion
  117.6 0.1 collective-permute-start.11
  117.7 14.6 %collective-permute-done.11 = bf16[2,2,48,512]{3,2,1,0:T(8,128)(2,1)S(1)} collective-permute-done((bf16[2,2,48,512]{3,2,1,0:T(8,128)(2,1)S(1)}, bf16[2,2,48,512]{3,2,1,0:T(8,128)(2,1)S(1)}, u32[]{:S(2)}, u32[]{:S(2)}) %collective-permute-start.11) | collective-permute-done | bytes 196640 | tf_op jit(solution)/shard_map/ppermute | solution.py:19
  132.3 0.1 fusion.1
  132.4 2.4 %collective-permute-start.12 = (bf16[2,48,512]{2,1,0:T(8,128)(2,1)S(1)}, bf16[2,48,512]{2,1,0:T(8,128)(2,1)S(1)}, u32[]{:S(2)}, u32[]{:S(2)}) collective-permute-start(bf16[2,48,512]{2,1,0:T(8,128)(2,1)S(1)} %get-tuple-element.155), channel_id=1, source_target_pairs={{0,4},{1,5},{2,6},{3,7},{4,0},{5,1},{6,2},{7,3},{8,12},{9,13},{10,... | collective-permute-start | bytes 294920 | tf_op jit(solution)/shard_map/ppermute | solution.py:19
  134.8 0.0 collective-permute-start.9
  134.8 3.5 %collective-permute-done.9.refs_1_ = s32[32]{0:T(128)S(1)} collective-permute-done((s32[32]{0:T(128)S(1)}, s32[32]{0:T(128)S(1)}, u32[]{:S(2)}, u32[]{:S(2)}) %collective-permute-start.9) | collective-permute-done | bytes 160 | tf_op jit(solution)/shard_map/ppermute | solution.py:19
  138.3 0.5 copy-done.6
  138.9 2.8 %shard_map.100 = (s32[64]{0:T(128)S(1)}, s32[64]{0:T(128)S(1)}, s32[64]{0:T(128)S(1)}, s32[1]{0:T(128)}) custom-call(s32[1]{0:T(128)} %bitcast.me_ref, s32[32]{0:T(128)} %get-tuple-element.137.refs_0_, s32[32]{0:T(128)} %copy-done.6), custom_call_target="tpu_custom_call" | custom-call | tf_op jit(solution)/shard_map/pallas_call | solution.py:131
  142.3 0.0 collective-permute-done.12
  142.3 0.0 all-to-all-done.4
  142.4 7.5 %conditional.1 = ((bf16[2,48,64,384]{3,2,1,0:T(8,128)(2,1)}, bf16[2,48,512]{2,1,0:T(8,128)(2,1)})) conditional(s32[]{:T(128)} %bitcast.4, (s32[64]{0:T(128)S(1)}, s32[64]{0:T(128)S(1)}, s32[64]{0:T(128)S(1)}, bf16[8,2,3,48,384]{4,3,2,1,0:T(8,128)(2,1)}, bf16[8,2,48,1408]{3,2,1,0:T(8,128)(2,1)}, ...), branch_computations={%region_0.1_spmd, %region_1.2_spmd, %region_2.3_spmd, %region_3.4_... | conditional | flops 5898240 | bytes 7471112 | solution.py:551
  142.4 7.5 %branch_0_fun.1 = (bf16[2,48,64,384]{3,2,1,0:T(8,128)(2,1)}, bf16[2,48,512]{2,1,0:T(8,128)(2,1)}) custom-call(s32[64]{0:T(128)S(1)} %get-tuple-element.62.order_ref, s32[64]{0:T(128)S(1)} %get-tuple-element.63.counts_ref, s32[64]{0:T(128)S(1)} %get-tuple-element.64.offsets_ref, bf16[8,2,3,48,384]{4,3,2,1,0:T(8,128)(2,1)} %get-tuple-element.65.whole_ref, ...), custom_call_target="tpu_custom_call" | custom-call | tf_op jit(solution)/shard_map/cond/branch_0_fun/pallas_call | solution.py:462
  (11 shorter events, 0.1 us)
Async XLA Ops:
  3.4 16.7 %collective-permute-start = (bf16[3,256,384]{2,1,0:T(8,128)(2,1)}, bf16[3,256,384]{2,1,0:T(8,128)(2,1)}, u32[]{:S(2)}, u32[]{:S(2)}) collective-permute-start(bf16[3,256,384]{2,1,0:T(8,128)(2,1)} %get-tuple-element.123.refs_5_), channel_id=1, source_target_pairs={{0,16},{8,24},{16,0},{24,8},{1,17},{9,25},{17,1},{25,9},{2,18},{10... | collective-permute-start | bytes 1769480 | tf_op jit(solution)/shard_map/ppermute | solution.py:19
  6.5 14.0 %collective-permute-start.2 = (bf16[3,256,384]{2,1,0:T(8,128)(2,1)}, bf16[3,256,384]{2,1,0:T(8,128)(2,1)}, u32[]{:S(2)}, u32[]{:S(2)}) collective-permute-start(bf16[3,256,384]{2,1,0:T(8,128)(2,1)} %get-tuple-element.123.refs_5_), channel_id=1, source_target_pairs={{0,8},{8,0},{16,24},{24,16},{1,9},{9,1},{17,25},{25,17},{2,10},{10... | collective-permute-start | bytes 1769480 | tf_op jit(solution)/shard_map/ppermute | solution.py:19
  20.1 2.3 %collective-permute-start.3 = (bf16[3,256,384]{2,1,0:T(8,128)(2,1)}, bf16[3,256,384]{2,1,0:T(8,128)(2,1)}, u32[]{:S(2)}, u32[]{:S(2)}) collective-permute-start(bf16[3,256,384]{2,1,0:T(8,128)(2,1)} %collective-permute-done.refs_7_), channel_id=1, source_target_pairs={{0,8},{8,0},{16,24},{24,16},{1,9},{9,1},{17,25},{25,17},{2,10},{10... | collective-permute-start | bytes 1769480 | tf_op jit(solution)/shard_map/ppermute | solution.py:19
  29.3 47.3 %all-to-all-start.3 = ((bf16[8,2,3,48,384]{4,3,2,1,0:T(8,128)(2,1)}), bf16[8,2,3,48,384]{4,3,2,1,0:T(8,128)(2,1)}, u32[]{:S(2)}, u32[]{:S(2)}) async-start(bf16[8,2,3,48,384]{4,3,2,1,0:T(8,128)(2,1)} %shard_map.96.tile_ref), calls=%async_computation.3 | async-start | bytes 3538944 | tf_op jit(solution)/shard_map/all_to_all | solution.py:522
  35.0 23.9 %copy-start.1 = (s32[8]{0:T(128)S(1)}, s32[8]{0:T(128)}, u32[]{:S(2)}) copy-start(s32[8]{0:T(128)} %refs_0_.1) | copy-start | bytes 100
  35.0 23.9 %collective-permute-start.1 = (bf16[5,256,384]{2,1,0:T(8,128)(2,1)}, bf16[5,256,384]{2,1,0:T(8,128)(2,1)}, u32[]{:S(2)}, u32[]{:S(2)}) collective-permute-start(bf16[5,256,384]{2,1,0:T(8,128)(2,1)} %get-tuple-element.124.refs_5_), channel_id=1, source_target_pairs={{0,16},{8,24},{16,0},{24,8},{1,17},{9,25},{17,1},{25,9},{2,18},{10... | collective-permute-start | bytes 2949128 | tf_op jit(solution)/shard_map/ppermute | solution.py:19
  36.6 26.7 %collective-permute-start.4 = (bf16[5,256,384]{2,1,0:T(8,128)(2,1)}, bf16[5,256,384]{2,1,0:T(8,128)(2,1)}, u32[]{:S(2)}, u32[]{:S(2)}) collective-permute-start(bf16[5,256,384]{2,1,0:T(8,128)(2,1)} %get-tuple-element.124.refs_5_), channel_id=1, source_target_pairs={{0,8},{8,0},{16,24},{24,16},{1,9},{9,1},{17,25},{25,17},{2,10},{10... | collective-permute-start | bytes 2949128 | tf_op jit(solution)/shard_map/ppermute | solution.py:19
  58.9 4.4 %collective-permute-start.5 = (bf16[5,256,384]{2,1,0:T(8,128)(2,1)}, bf16[5,256,384]{2,1,0:T(8,128)(2,1)}, u32[]{:S(2)}, u32[]{:S(2)}) collective-permute-start(bf16[5,256,384]{2,1,0:T(8,128)(2,1)} %collective-permute-done.1.refs_7_), channel_id=1, source_target_pairs={{0,8},{8,0},{16,24},{24,16},{1,9},{9,1},{17,25},{25,17},{2,10},{10... | collective-permute-start | bytes 2949128 | tf_op jit(solution)/shard_map/ppermute | solution.py:19
  58.9 15.4 %collective-permute-start.6 = (s32[8]{0:T(128)S(1)}, s32[8]{0:T(128)S(1)}, u32[]{:S(2)}, u32[]{:S(2)}) collective-permute-start(s32[8]{0:T(128)S(1)} %copy-done.1), channel_id=1, source_target_pairs={{0,2},{1,3},{2,0},{3,1},{4,6},{5,7},{6,4},{7,5},{8,10},{9,11},{10,... | collective-permute-start | bytes 104 | tf_op jit(solution)/shard_map/ppermute | solution.py:19
  60.6 16.1 %collective-permute-start.7 = (s32[8]{0:T(128)S(1)}, s32[8]{0:T(128)S(1)}, u32[]{:S(2)}, u32[]{:S(2)}) collective-permute-start(s32[8]{0:T(128)S(1)} %copy-done.1), channel_id=1, source_target_pairs={{0,4},{1,5},{2,6},{3,7},{4,0},{5,1},{6,2},{7,3},{8,12},{9,13},{10,... | collective-permute-start | bytes 104 | tf_op jit(solution)/shard_map/ppermute | solution.py:19
  62.9 13.7 %collective-permute-start.8 = (s32[8]{0:T(128)S(1)}, s32[8]{0:T(128)S(1)}, u32[]{:S(2)}, u32[]{:S(2)}) collective-permute-start(s32[8]{0:T(128)S(1)} %copy-done.1), channel_id=1, source_target_pairs={{0,6},{1,7},{2,4},{3,5},{4,2},{5,3},{6,0},{7,1},{8,14},{9,15},{10,... | collective-permute-start | bytes 104 | tf_op jit(solution)/shard_map/ppermute | solution.py:19
  74.3 7.0 %copy-start.2 = (s32[8]{0:T(128)}, s32[8]{0:T(128)S(1)}, u32[]{:S(2)}) copy-start(s32[8]{0:T(128)S(1)} %collective-permute-done.6.refs_1_) | copy-start | bytes 100
  76.6 4.6 %copy-start.3 = (s32[8]{0:T(128)}, s32[8]{0:T(128)S(1)}, u32[]{:S(2)}) copy-start(s32[8]{0:T(128)S(1)} %collective-permute-done.7.refs_2_) | copy-start | bytes 100
  76.6 4.6 %copy-start.4 = (s32[8]{0:T(128)}, s32[8]{0:T(128)S(1)}, u32[]{:S(2)}) copy-start(s32[8]{0:T(128)S(1)} %collective-permute-done.8.refs_3_) | copy-start | bytes 100
  76.6 65.7 %all-to-all-start.4 = ((bf16[8,2,48,1408]{3,2,1,0:T(8,128)(2,1)}), bf16[8,2,48,1408]{3,2,1,0:T(8,128)(2,1)}, u32[]{:S(2)}, u32[]{:S(2)}) async-start(bf16[8,2,48,1408]{3,2,1,0:T(8,128)(2,1)} %get-tuple-element.132), calls=%async_computation.4 | async-start | bytes 4325376 | tf_op jit(solution)/shard_map/all_to_all | solution.py:533
  94.9 39.9 %copy-start.5 = (s32[32]{0:T(128)S(1)}, s32[32]{0:T(128)}, u32[]{:S(2)}) copy-start(s32[32]{0:T(128)} %get-tuple-element.137.refs_0_) | copy-start | bytes 388
  94.9 47.4 %copy-start = (bf16[8,2,48,512]{3,2,1,0:T(8,128)(2,1)S(1)}, bf16[8,2,48,512]{3,2,1,0:T(8,128)(2,1)}, u32[]{:S(2)}) copy-start(bf16[8,2,48,512]{3,2,1,0:T(8,128)(2,1)} %get-tuple-element.144) | copy-start | bytes 2359300
  96.0 20.4 %collective-permute-start.10 = (bf16[4,2,48,512]{3,2,1,0:T(8,128)(2,1)S(1)}, bf16[4,2,48,512]{3,2,1,0:T(8,128)(2,1)S(1)}, u32[]{:S(2)}, u32[]{:S(2)}) collective-permute-start(bf16[4,2,48,512]{3,2,1,0:T(8,128)(2,1)S(1)} %dynamic-slice_bitcast_fusion), channel_id=1, source_target_pairs={{0,1},{1,0},{2,3},{3,2},{4,5},{5,4},{6,7},{7,6},{8,9},{9,8},{10,11... | collective-permute-start | bytes 1179656 | tf_op jit(solution)/shard_map/ppermute | solution.py:19
  117.6 14.7 %collective-permute-start.11 = (bf16[2,2,48,512]{3,2,1,0:T(8,128)(2,1)S(1)}, bf16[2,2,48,512]{3,2,1,0:T(8,128)(2,1)S(1)}, u32[]{:S(2)}, u32[]{:S(2)}) collective-permute-start(bf16[2,2,48,512]{3,2,1,0:T(8,128)(2,1)S(1)} %dynamic-slice_bitcast_fusion.1), channel_id=1, source_target_pairs={{0,2},{1,3},{2,0},{3,1},{4,6},{5,7},{6,4},{7,5},{8,10},{9,11},{10,... | collective-permute-start | bytes 589832 | tf_op jit(solution)/shard_map/ppermute | solution.py:19
  132.4 9.9 %collective-permute-start.12 = (bf16[2,48,512]{2,1,0:T(8,128)(2,1)S(1)}, bf16[2,48,512]{2,1,0:T(8,128)(2,1)S(1)}, u32[]{:S(2)}, u32[]{:S(2)}) collective-permute-start(bf16[2,48,512]{2,1,0:T(8,128)(2,1)S(1)} %get-tuple-element.155), channel_id=1, source_target_pairs={{0,4},{1,5},{2,6},{3,7},{4,0},{5,1},{6,2},{7,3},{8,12},{9,13},{10,... | collective-permute-start | bytes 294920 | tf_op jit(solution)/shard_map/ppermute | solution.py:19
  134.8 3.5 %collective-permute-start.9 = (s32[32]{0:T(128)S(1)}, s32[32]{0:T(128)S(1)}, u32[]{:S(2)}, u32[]{:S(2)}) collective-permute-start(s32[32]{0:T(128)S(1)} %copy-done.5), channel_id=1, source_target_pairs={{0,1},{1,0},{2,3},{3,2},{4,5},{5,4},{6,7},{7,6},{8,9},{9,8},{10,11... | collective-permute-start | bytes 392 | tf_op jit(solution)/shard_map/ppermute | solution.py:19
  138.3 0.5 copy-start.6

commit v2 on v1

--- a/solution.py
+++ b/solution.py
@@ -30,7 +30,7 @@
     size = lax.axis_size(axis)
     me = lax.axis_index(axis)
     held, bit = total, 1
-    while held.shape[0] > 2:
+    while held.shape[0] > 4:
         pairs = held.reshape((held.shape[0] // 2, 2) + held.shape[1:])
         mine = (me // bit) % 2
         keep = lax.dynamic_index_in_dim(pairs, mine, 1, keepdims=False)

time: 151 us -> 146 us (0.967)
  waiting for transfers between devices: 43.9 us -> 35 us
  starting transfers between devices: 23.7 us -> 28.5 us
    ppermute x13 -> x14, waiting for transfers between devices: 43.9 us -> 35 us  [exchange(): return lax.ppermute(x, axis, [(a, a ^ flip) for a in range(size)])]
    ppermute x13 -> x14, starting transfers between devices: 13.6 us -> 17.9 us  [exchange(): return lax.ppermute(x, axis, [(a, a ^ flip) for a in range(size)])]
  transfers between devices with their start and end apart: 15 -> 16, of which waited for: 7 -> 7; matrix products, arithmetic and copies ran while one was open for 2% -> 1% of each run, Pallas kernels for 40% -> 42%
where the time goes in v2:
time: 146 us; the launch traced here: 145 us
  Pallas kernels  77.9 us (53%)
  waiting for transfers between devices  35 us (24%)
  starting transfers between devices  28.5 us (20%)
  local copies, waits for them, and re-layouts  1.59 us (1%)
  between operations  1.48 us (1%)
    ppermute x14, waiting for transfers between devices, exchange(): return lax.ppermute(x, axis, [(a, a ^ flip) for a in range(size)])  35 us
    pallas_call x2, Pallas kernels, left_products(): pl.pallas_call(functools.partial(left_kernel, nshard, first), grid_spec=p...  33.2 us
    ppermute x14, starting transfers between devices, exchange(): return lax.ppermute(x, axis, [(a, a ^ flip) for a in range(size)])  17.9 us
    pallas_call x2, Pallas kernels, tiles(): pl.pallas_call(functools.partial(tile_kernel, nshard, first, packed), gri...  17.9 us
    pallas_call x2, Pallas kernels, project(): pl.pallas_call(functools.partial(project_kernel, started), grid_spec=pltp...  13.7 us
    pallas_call x1, Pallas kernels, unpack(): pl.pallas_call(functools.partial(unpack_kernel, cut), grid_spec=pltpu.Pre...  7.55 us
    all_to_all x1, starting transfers between devices, body(): lax.all_to_all(tiles_a, 'src', split_axis=0, concat_axis=0, tiled=True)  6.02 us
    all_to_all x1, starting transfers between devices, body(): lax.all_to_all(packed, 'src', split_axis=0, concat_axis=0, tiled=True)  4.54 us
  transfers between devices with their start and end apart: 16, of which 7 were waited for; matrix products, arithmetic and copies ran while one was open for 1% of the time, Pallas kernels for 42%

profile of v2, /device:TPU:0, one launch (start us, length us, event | category | flops | bytes accessed | tf_op | source)
XLA Modules:
  0.0 145.5 jit_solution(1230062948375157571)
XLA Ops:
  0.6 2.8 %shard_map.94 = (s32[8]{0:T(128)}, s32[8]{0:T(128)}, bf16[3,256,384]{2,1,0:T(8,128)(2,1)}, bf16[5,256,384]{2,1,0:T(8,128)(2,1)}) custom-call(s32[8]{0:T(128)} %refs_0_.1, bf16[8,256,384]{2,1,0:T(8,128)(2,1)} %basis_ref.3), custom_call_target="tpu_custom_call" | custom-call | tf_op jit(solution)/shard_map/pallas_call | solution.py:85
  3.4 3.0 %collective-permute-start = (bf16[3,256,384]{2,1,0:T(8,128)(2,1)}, bf16[3,256,384]{2,1,0:T(8,128)(2,1)}, u32[]{:S(2)}, u32[]{:S(2)}) collective-permute-start(bf16[3,256,384]{2,1,0:T(8,128)(2,1)} %get-tuple-element.147.refs_5_), channel_id=1, source_target_pairs={{0,16},{8,24},{16,0},{24,8},{1,17},{9,25},{17,1},{25,9},{2,18},{10... | collective-permute-start | bytes 1769480 | tf_op jit(solution)/shard_map/ppermute | solution.py:19
  6.5 0.0 collective-permute-start.2
  6.5 13.5 %shard_map.95.refs_4_ = bf16[2,3,384,1024]{3,2,1,0:T(8,128)(2,1)} custom-call(s32[1]{0:T(128)} %bitcast.1.me_ref, s32[8]{0:T(128)} %get-tuple-element.144.order_ref.refs_0_, f32[3,2,1024]{2,1,0:T(2,128)} %bitcast.23, f32[3,8,1024]{2,1,0:T(8,128)} %bitcast.21, bf16[2,1024,384]{2,1,0:T(8,128)(2,1)} %basis_ref.5), custom_call_target="tpu_custom_call" | custom-call | flops 4831838208 | bytes 4718592 | tf_op jit(solution)/shard_map/pallas_call | solution.py:213
  20.0 0.2 collective-permute-done.refs_7_
  20.1 0.3 collective-permute-start.3
  20.5 0.0 collective-permute-done.2.refs_6_
  20.5 2.0 %collective-permute-done.3.refs_8_ = bf16[3,256,384]{2,1,0:T(8,128)(2,1)} collective-permute-done((bf16[3,256,384]{2,1,0:T(8,128)(2,1)}, bf16[3,256,384]{2,1,0:T(8,128)(2,1)}, u32[]{:S(2)}, u32[]{:S(2)}) %collective-permute-start.3) | collective-permute-done | bytes 589856 | tf_op jit(solution)/shard_map/ppermute | solution.py:19
  22.5 6.9 %shard_map.96.tile_ref = bf16[8,2,3,48,384]{4,3,2,1,0:T(8,128)(2,1)} custom-call(s32[8]{0:T(128)} %get-tuple-element.144.order_ref.refs_0_, s32[8]{0:T(128)} %refs_0_.1, s32[8]{0:T(128)} %get-tuple-element.145.refs_2_, s32[2]{0:T(128)} %refs_3_.3, bf16[2,3,384,1024]{3,2,1,0:T(8,128)(2,1)} %shard_map.95.refs_4_, ...), custom_call_target="tpu_custom_call" | custom-call | flops 1811939328 | bytes 6488064 | tf_op jit(solution)/shard_map/pallas_call | solution.py:321
  29.4 6.0 %all-to-all-start.3 = ((bf16[8,2,3,48,384]{4,3,2,1,0:T(8,128)(2,1)}), bf16[8,2,3,48,384]{4,3,2,1,0:T(8,128)(2,1)}, u32[]{:S(2)}, u32[]{:S(2)}) async-start(bf16[8,2,3,48,384]{4,3,2,1,0:T(8,128)(2,1)} %shard_map.96.tile_ref), calls=%async_computation.3 | async-start | bytes 3538944 | tf_op jit(solution)/shard_map/all_to_all | solution.py:522
  35.4 1.6 %collective-permute-start.1 = (bf16[5,256,384]{2,1,0:T(8,128)(2,1)}, bf16[5,256,384]{2,1,0:T(8,128)(2,1)}, u32[]{:S(2)}, u32[]{:S(2)}) collective-permute-start(bf16[5,256,384]{2,1,0:T(8,128)(2,1)} %get-tuple-element.148.refs_5_), channel_id=1, source_target_pairs={{0,16},{8,24},{16,0},{24,8},{1,17},{9,25},{17,1},{25,9},{2,18},{10... | collective-permute-start | bytes 2949128 | tf_op jit(solution)/shard_map/ppermute | solution.py:19
  37.0 0.0 collective-permute-start.4
  37.0 19.7 %shard_map.97.refs_4_ = bf16[2,5,384,1024]{3,2,1,0:T(8,128)(2,1)} custom-call(s32[1]{0:T(128)} %bitcast.1.me_ref, s32[8]{0:T(128)} %get-tuple-element.144.order_ref.refs_0_, f32[3,2,1024]{2,1,0:T(2,128)} %bitcast.24, f32[3,8,1024]{2,1,0:T(8,128)} %bitcast.22, bf16[2,1024,384]{2,1,0:T(8,128)(2,1)} %basis_ref.5), custom_call_target="tpu_custom_call" | custom-call | flops 8053063680 | bytes 7864320 | tf_op jit(solution)/shard_map/pallas_call | solution.py:213
  56.7 2.6 %collective-permute-done.1.refs_7_ = bf16[5,256,384]{2,1,0:T(8,128)(2,1)} collective-permute-done((bf16[5,256,384]{2,1,0:T(8,128)(2,1)}, bf16[5,256,384]{2,1,0:T(8,128)(2,1)}, u32[]{:S(2)}, u32[]{:S(2)}) %collective-permute-start.1) | collective-permute-done | bytes 983072 | tf_op jit(solution)/shard_map/ppermute | solution.py:19
  59.3 0.0 collective-permute-start.5
  59.3 0.0 copy-done
  59.3 1.7 %collective-permute-start.6 = (s32[8]{0:T(128)S(1)}, s32[8]{0:T(128)S(1)}, u32[]{:S(2)}, u32[]{:S(2)}) collective-permute-start(s32[8]{0:T(128)S(1)} %copy-done), channel_id=1, source_target_pairs={{0,2},{1,3},{2,0},{3,1},{4,6},{5,7},{6,4},{7,5},{8,10},{9,11},{10,... | collective-permute-start | bytes 104 | tf_op jit(solution)/shard_map/ppermute | solution.py:19
  61.0 2.4 %collective-permute-start.7 = (s32[8]{0:T(128)S(1)}, s32[8]{0:T(128)S(1)}, u32[]{:S(2)}, u32[]{:S(2)}) collective-permute-start(s32[8]{0:T(128)S(1)} %copy-done), channel_id=1, source_target_pairs={{0,4},{1,5},{2,6},{3,7},{4,0},{5,1},{6,2},{7,3},{8,12},{9,13},{10,... | collective-permute-start | bytes 104 | tf_op jit(solution)/shard_map/ppermute | solution.py:19
  63.3 0.3 collective-permute-start.8
  63.7 0.0 collective-permute-done.4.refs_6_
  63.7 0.0 collective-permute-done.5.refs_8_
  63.7 11.0 %shard_map.98 = (bf16[8,2,5,48,384]{4,3,2,1,0:T(8,128)(2,1)}, bf16[8,2,48,1408]{3,2,1,0:T(8,128)(2,1)}, bf16[8,2,48,512]{3,2,1,0:T(8,128)(2,1)}) custom-call(s32[8]{0:T(128)} %get-tuple-element.144.order_ref.refs_0_, s32[8]{0:T(128)} %refs_0_.1, s32[8]{0:T(128)} %get-tuple-element.145.refs_2_, s32[2]{0:T(128)} %refs_3_.3, ...), custom_call_target="tpu_custom_call" | custom-call | flops 3019898880 | bytes 10813440 | tf_op jit(solution)/shard_map/pallas_call | solution.py:321
  74.7 0.0 collective-permute-done.6.refs_1_
  74.7 0.0 copy-start.1
  74.7 2.4 %collective-permute-done.7.refs_2_ = s32[8]{0:T(128)S(1)} collective-permute-done((s32[8]{0:T(128)S(1)}, s32[8]{0:T(128)S(1)}, u32[]{:S(2)}, u32[]{:S(2)}) %collective-permute-start.7) | collective-permute-done | bytes 64 | tf_op jit(solution)/shard_map/ppermute | solution.py:19
  77.0 0.0 collective-permute-done.8.refs_3_
  77.1 0.0 all-to-all-done.3
  77.1 4.5 %all-to-all-start.4 = ((bf16[8,2,48,1408]{3,2,1,0:T(8,128)(2,1)}), bf16[8,2,48,1408]{3,2,1,0:T(8,128)(2,1)}, u32[]{:S(2)}, u32[]{:S(2)}) async-start(bf16[8,2,48,1408]{3,2,1,0:T(8,128)(2,1)} %get-tuple-element.156), calls=%async_computation.4 | async-start | bytes 4325376 | tf_op jit(solution)/shard_map/all_to_all | solution.py:533
  81.6 0.0 copy-done.1
  81.7 5.7 %shard_map.99 = (f32[768,512]{1,0:T(8,128)}, s32[32]{0:T(128)}) custom-call(s32[8]{0:T(128)} %get-tuple-element.144.order_ref.refs_0_, bf16[8,2,3,48,384]{4,3,2,1,0:T(8,128)(2,1)} %shard_map.96.tile_ref, bf16[8,384,512]{2,1,0:T(8,128)(2,1)} %coeff_ref.3, s32[8]{0:T(128)} %refs_0_.1, s32[8]{0:T(128)} %copy-done.1, s32[8]{0:T(128)} %copy-done.2, s32[8]{0:T(128)} %copy-done.3), custom_call_target="tpu_custom_call" | custom-call | flops 905969664 | bytes 1769472 | tf_op jit(solution)/shard_map/pallas_call | solution.py:391
  87.4 7.9 %shard_map.101 = bf16[8,2,48,512]{3,2,1,0:T(8,128)(2,1)} custom-call(s32[8]{0:T(128)} %get-tuple-element.144.order_ref.refs_0_, bf16[8,2,5,48,384]{4,3,2,1,0:T(8,128)(2,1)} %get-tuple-element.166.tile_ref, bf16[8,384,512]{2,1,0:T(8,128)(2,1)} %coeff_ref.3, f32[768,512]{1,0:T(8,128)} %get-tuple-element.167.refs_0_), custom_call_target="tpu_custom_call" | custom-call | flops 1509949440 | bytes 2949120 | tf_op jit(solution)/shard_map/pallas_call | solution.py:391
  95.4 1.0 dynamic-slice_bitcast_fusion
  96.4 1.7 %collective-permute-start.10 = (bf16[4,2,48,512]{3,2,1,0:T(8,128)(2,1)S(1)}, bf16[4,2,48,512]{3,2,1,0:T(8,128)(2,1)S(1)}, u32[]{:S(2)}, u32[]{:S(2)}) collective-permute-start(bf16[4,2,48,512]{3,2,1,0:T(8,128)(2,1)S(1)} %dynamic-slice_bitcast_fusion), channel_id=1, source_target_pairs={{0,1},{1,0},{2,3},{3,2},{4,5},{5,4},{6,7},{7,6},{8,9},{9,8},{10,11... | collective-permute-start | bytes 1179656 | tf_op jit(solution)/shard_map/ppermute | solution.py:19
  98.1 18.7 %collective-permute-done.10 = bf16[4,2,48,512]{3,2,1,0:T(8,128)(2,1)S(1)} collective-permute-done((bf16[4,2,48,512]{3,2,1,0:T(8,128)(2,1)S(1)}, bf16[4,2,48,512]{3,2,1,0:T(8,128)(2,1)S(1)}, u32[]{:S(2)}, u32[]{:S(2)}) %collective-permute-start.10) | collective-permute-done | bytes 393248 | tf_op jit(solution)/shard_map/ppermute | solution.py:19
  116.8 1.1 fusion
  118.0 0.1 collective-permute-start.11
  118.1 6.7 %collective-permute-start.12 = (bf16[2,48,512]{2,1,0:T(8,128)(2,1)S(1)}, bf16[2,48,512]{2,1,0:T(8,128)(2,1)S(1)}, u32[]{:S(2)}, u32[]{:S(2)}) collective-permute-start(bf16[2,48,512]{2,1,0:T(8,128)(2,1)S(1)} %get-tuple-element.180), channel_id=1, source_target_pairs={{0,4},{1,5},{2,6},{3,7},{4,0},{5,1},{6,2},{7,3},{8,12},{9,13},{10,... | collective-permute-start | bytes 294920 | tf_op jit(solution)/shard_map/ppermute | solution.py:19
  124.8 0.0 collective-permute-start.13
  124.8 0.0 collective-permute-start.9
  124.8 3.5 %collective-permute-done.9.refs_1_ = s32[32]{0:T(128)S(1)} collective-permute-done((s32[32]{0:T(128)S(1)}, s32[32]{0:T(128)S(1)}, u32[]{:S(2)}, u32[]{:S(2)}) %collective-permute-start.9) | collective-permute-done | bytes 160 | tf_op jit(solution)/shard_map/ppermute | solution.py:19
  128.3 0.5 copy-done.5
  128.9 2.8 %shard_map.100 = (s32[64]{0:T(128)S(1)}, s32[64]{0:T(128)S(1)}, s32[64]{0:T(128)S(1)}, s32[1]{0:T(128)}) custom-call(s32[1]{0:T(128)} %bitcast.me_ref, s32[32]{0:T(128)} %get-tuple-element.161.refs_0_, s32[32]{0:T(128)} %copy-done.5), custom_call_target="tpu_custom_call" | custom-call | tf_op jit(solution)/shard_map/pallas_call | solution.py:131
  132.3 0.0 collective-permute-done.11
  132.3 5.6 %collective-permute-done.12 = bf16[2,48,512]{2,1,0:T(8,128)(2,1)S(1)} collective-permute-done((bf16[2,48,512]{2,1,0:T(8,128)(2,1)S(1)}, bf16[2,48,512]{2,1,0:T(8,128)(2,1)S(1)}, u32[]{:S(2)}, u32[]{:S(2)}) %collective-permute-start.12) | collective-permute-done | bytes 98336 | tf_op jit(solution)/shard_map/ppermute | solution.py:19
  137.9 0.0 collective-permute-done.13
  137.9 0.0 all-to-all-done.4
  137.9 7.5 %conditional.1 = ((bf16[2,48,64,384]{3,2,1,0:T(8,128)(2,1)}, bf16[2,48,512]{2,1,0:T(8,128)(2,1)})) conditional(s32[]{:T(128)} %bitcast.4, (s32[64]{0:T(128)S(1)}, s32[64]{0:T(128)S(1)}, s32[64]{0:T(128)S(1)}, bf16[8,2,3,48,384]{4,3,2,1,0:T(8,128)(2,1)}, bf16[8,2,48,1408]{3,2,1,0:T(8,128)(2,1)}, ...), branch_computations={%region_0.1_spmd, %region_1.2_spmd, %region_2.3_spmd, %region_3.4_... | conditional | flops 5898240 | bytes 7471112 | solution.py:551
  137.9 7.5 %branch_0_fun.1 = (bf16[2,48,64,384]{3,2,1,0:T(8,128)(2,1)}, bf16[2,48,512]{2,1,0:T(8,128)(2,1)}) custom-call(s32[64]{0:T(128)S(1)} %get-tuple-element.78.order_ref, s32[64]{0:T(128)S(1)} %get-tuple-element.79.counts_ref, s32[64]{0:T(128)S(1)} %get-tuple-element.80.offsets_ref, bf16[8,2,3,48,384]{4,3,2,1,0:T(8,128)(2,1)} %get-tuple-element.81.whole_ref, ...), custom_call_target="tpu_custom_call" | custom-call | tf_op jit(solution)/shard_map/cond/branch_0_fun/pallas_call | solution.py:462
  (9 shorter events, 0.1 us)
Async XLA Ops:
  3.4 16.7 %collective-permute-start = (bf16[3,256,384]{2,1,0:T(8,128)(2,1)}, bf16[3,256,384]{2,1,0:T(8,128)(2,1)}, u32[]{:S(2)}, u32[]{:S(2)}) collective-permute-start(bf16[3,256,384]{2,1,0:T(8,128)(2,1)} %get-tuple-element.147.refs_5_), channel_id=1, source_target_pairs={{0,16},{8,24},{16,0},{24,8},{1,17},{9,25},{17,1},{25,9},{2,18},{10... | collective-permute-start | bytes 1769480 | tf_op jit(solution)/shard_map/ppermute | solution.py:19
  6.5 14.0 %collective-permute-start.2 = (bf16[3,256,384]{2,1,0:T(8,128)(2,1)}, bf16[3,256,384]{2,1,0:T(8,128)(2,1)}, u32[]{:S(2)}, u32[]{:S(2)}) collective-permute-start(bf16[3,256,384]{2,1,0:T(8,128)(2,1)} %get-tuple-element.147.refs_5_), channel_id=1, source_target_pairs={{0,8},{8,0},{16,24},{24,16},{1,9},{9,1},{17,25},{25,17},{2,10},{10... | collective-permute-start | bytes 1769480 | tf_op jit(solution)/shard_map/ppermute | solution.py:19
  20.1 2.3 %collective-permute-start.3 = (bf16[3,256,384]{2,1,0:T(8,128)(2,1)}, bf16[3,256,384]{2,1,0:T(8,128)(2,1)}, u32[]{:S(2)}, u32[]{:S(2)}) collective-permute-start(bf16[3,256,384]{2,1,0:T(8,128)(2,1)} %collective-permute-done.refs_7_), channel_id=1, source_target_pairs={{0,8},{8,0},{16,24},{24,16},{1,9},{9,1},{17,25},{25,17},{2,10},{10... | collective-permute-start | bytes 1769480 | tf_op jit(solution)/shard_map/ppermute | solution.py:19
  29.4 47.7 %all-to-all-start.3 = ((bf16[8,2,3,48,384]{4,3,2,1,0:T(8,128)(2,1)}), bf16[8,2,3,48,384]{4,3,2,1,0:T(8,128)(2,1)}, u32[]{:S(2)}, u32[]{:S(2)}) async-start(bf16[8,2,3,48,384]{4,3,2,1,0:T(8,128)(2,1)} %shard_map.96.tile_ref), calls=%async_computation.3 | async-start | bytes 3538944 | tf_op jit(solution)/shard_map/all_to_all | solution.py:522
  35.4 23.9 %copy-start = (s32[8]{0:T(128)S(1)}, s32[8]{0:T(128)}, u32[]{:S(2)}) copy-start(s32[8]{0:T(128)} %refs_0_.1) | copy-start | bytes 100
  35.4 23.9 %collective-permute-start.1 = (bf16[5,256,384]{2,1,0:T(8,128)(2,1)}, bf16[5,256,384]{2,1,0:T(8,128)(2,1)}, u32[]{:S(2)}, u32[]{:S(2)}) collective-permute-start(bf16[5,256,384]{2,1,0:T(8,128)(2,1)} %get-tuple-element.148.refs_5_), channel_id=1, source_target_pairs={{0,16},{8,24},{16,0},{24,8},{1,17},{9,25},{17,1},{25,9},{2,18},{10... | collective-permute-start | bytes 2949128 | tf_op jit(solution)/shard_map/ppermute | solution.py:19
  37.0 26.7 %collective-permute-start.4 = (bf16[5,256,384]{2,1,0:T(8,128)(2,1)}, bf16[5,256,384]{2,1,0:T(8,128)(2,1)}, u32[]{:S(2)}, u32[]{:S(2)}) collective-permute-start(bf16[5,256,384]{2,1,0:T(8,128)(2,1)} %get-tuple-element.148.refs_5_), channel_id=1, source_target_pairs={{0,8},{8,0},{16,24},{24,16},{1,9},{9,1},{17,25},{25,17},{2,10},{10... | collective-permute-start | bytes 2949128 | tf_op jit(solution)/shard_map/ppermute | solution.py:19
  59.3 4.4 %collective-permute-start.5 = (bf16[5,256,384]{2,1,0:T(8,128)(2,1)}, bf16[5,256,384]{2,1,0:T(8,128)(2,1)}, u32[]{:S(2)}, u32[]{:S(2)}) collective-permute-start(bf16[5,256,384]{2,1,0:T(8,128)(2,1)} %collective-permute-done.1.refs_7_), channel_id=1, source_target_pairs={{0,8},{8,0},{16,24},{24,16},{1,9},{9,1},{17,25},{25,17},{2,10},{10... | collective-permute-start | bytes 2949128 | tf_op jit(solution)/shard_map/ppermute | solution.py:19
  59.3 15.4 %collective-permute-start.6 = (s32[8]{0:T(128)S(1)}, s32[8]{0:T(128)S(1)}, u32[]{:S(2)}, u32[]{:S(2)}) collective-permute-start(s32[8]{0:T(128)S(1)} %copy-done), channel_id=1, source_target_pairs={{0,2},{1,3},{2,0},{3,1},{4,6},{5,7},{6,4},{7,5},{8,10},{9,11},{10,... | collective-permute-start | bytes 104 | tf_op jit(solution)/shard_map/ppermute | solution.py:19
  61.0 16.1 %collective-permute-start.7 = (s32[8]{0:T(128)S(1)}, s32[8]{0:T(128)S(1)}, u32[]{:S(2)}, u32[]{:S(2)}) collective-permute-start(s32[8]{0:T(128)S(1)} %copy-done), channel_id=1, source_target_pairs={{0,4},{1,5},{2,6},{3,7},{4,0},{5,1},{6,2},{7,3},{8,12},{9,13},{10,... | collective-permute-start | bytes 104 | tf_op jit(solution)/shard_map/ppermute | solution.py:19
  63.3 13.7 %collective-permute-start.8 = (s32[8]{0:T(128)S(1)}, s32[8]{0:T(128)S(1)}, u32[]{:S(2)}, u32[]{:S(2)}) collective-permute-start(s32[8]{0:T(128)S(1)} %copy-done), channel_id=1, source_target_pairs={{0,6},{1,7},{2,4},{3,5},{4,2},{5,3},{6,0},{7,1},{8,14},{9,15},{10,... | collective-permute-start | bytes 104 | tf_op jit(solution)/shard_map/ppermute | solution.py:19
  74.7 7.0 %copy-start.1 = (s32[8]{0:T(128)}, s32[8]{0:T(128)S(1)}, u32[]{:S(2)}) copy-start(s32[8]{0:T(128)S(1)} %collective-permute-done.6.refs_1_) | copy-start | bytes 100
  77.0 4.6 %copy-start.2 = (s32[8]{0:T(128)}, s32[8]{0:T(128)S(1)}, u32[]{:S(2)}) copy-start(s32[8]{0:T(128)S(1)} %collective-permute-done.7.refs_2_) | copy-start | bytes 100
  77.0 4.6 %copy-start.3 = (s32[8]{0:T(128)}, s32[8]{0:T(128)S(1)}, u32[]{:S(2)}) copy-start(s32[8]{0:T(128)S(1)} %collective-permute-done.8.refs_3_) | copy-start | bytes 100
  77.1 60.9 %all-to-all-start.4 = ((bf16[8,2,48,1408]{3,2,1,0:T(8,128)(2,1)}), bf16[8,2,48,1408]{3,2,1,0:T(8,128)(2,1)}, u32[]{:S(2)}, u32[]{:S(2)}) async-start(bf16[8,2,48,1408]{3,2,1,0:T(8,128)(2,1)} %get-tuple-element.156), calls=%async_computation.4 | async-start | bytes 4325376 | tf_op jit(solution)/shard_map/all_to_all | solution.py:533
  87.4 37.4 %copy-start.4 = (s32[32]{0:T(128)S(1)}, s32[32]{0:T(128)}, u32[]{:S(2)}) copy-start(s32[32]{0:T(128)} %get-tuple-element.161.refs_0_) | copy-start | bytes 388
  96.4 20.4 %collective-permute-start.10 = (bf16[4,2,48,512]{3,2,1,0:T(8,128)(2,1)S(1)}, bf16[4,2,48,512]{3,2,1,0:T(8,128)(2,1)S(1)}, u32[]{:S(2)}, u32[]{:S(2)}) collective-permute-start(bf16[4,2,48,512]{3,2,1,0:T(8,128)(2,1)S(1)} %dynamic-slice_bitcast_fusion), channel_id=1, source_target_pairs={{0,1},{1,0},{2,3},{3,2},{4,5},{5,4},{6,7},{7,6},{8,9},{9,8},{10,11... | collective-permute-start | bytes 1179656 | tf_op jit(solution)/shard_map/ppermute | solution.py:19
  118.0 14.4 %collective-permute-start.11 = (bf16[2,48,512]{2,1,0:T(8,128)(2,1)S(1)}, bf16[2,48,512]{2,1,0:T(8,128)(2,1)S(1)}, u32[]{:S(2)}, u32[]{:S(2)}) collective-permute-start(bf16[2,48,512]{2,1,0:T(8,128)(2,1)S(1)} %get-tuple-element.181), channel_id=1, source_target_pairs={{0,2},{1,3},{2,0},{3,1},{4,6},{5,7},{6,4},{7,5},{8,10},{9,11},{10,... | collective-permute-start | bytes 294920 | tf_op jit(solution)/shard_map/ppermute | solution.py:19
  118.1 19.9 %collective-permute-start.12 = (bf16[2,48,512]{2,1,0:T(8,128)(2,1)S(1)}, bf16[2,48,512]{2,1,0:T(8,128)(2,1)S(1)}, u32[]{:S(2)}, u32[]{:S(2)}) collective-permute-start(bf16[2,48,512]{2,1,0:T(8,128)(2,1)S(1)} %get-tuple-element.180), channel_id=1, source_target_pairs={{0,4},{1,5},{2,6},{3,7},{4,0},{5,1},{6,2},{7,3},{8,12},{9,13},{10,... | collective-permute-start | bytes 294920 | tf_op jit(solution)/shard_map/ppermute | solution.py:19
  124.8 13.1 %collective-permute-start.13 = (bf16[2,48,512]{2,1,0:T(8,128)(2,1)S(1)}, bf16[2,48,512]{2,1,0:T(8,128)(2,1)S(1)}, u32[]{:S(2)}, u32[]{:S(2)}) collective-permute-start(bf16[2,48,512]{2,1,0:T(8,128)(2,1)S(1)} %get-tuple-element.179), channel_id=1, source_target_pairs={{0,6},{1,7},{2,4},{3,5},{4,2},{5,3},{6,0},{7,1},{8,14},{9,15},{10,... | collective-permute-start | bytes 294920 | tf_op jit(solution)/shard_map/ppermute | solution.py:19
  124.8 3.5 %collective-permute-start.9 = (s32[32]{0:T(128)S(1)}, s32[32]{0:T(128)S(1)}, u32[]{:S(2)}, u32[]{:S(2)}) collective-permute-start(s32[32]{0:T(128)S(1)} %copy-done.4), channel_id=1, source_target_pairs={{0,1},{1,0},{2,3},{3,2},{4,5},{5,4},{6,7},{7,6},{8,9},{9,8},{10,11... | collective-permute-start | bytes 392 | tf_op jit(solution)/shard_map/ppermute | solution.py:19
  128.3 0.5 copy-start.5

commit v3 on v2

--- a/solution.py
+++ b/solution.py
@@ -137,7 +137,7 @@
     )(me, *groups)
 
 
-NFEATURE = 128
+NFEATURE = 64
 
 
 def fill_features(rows_ref, points, is_test):
@@ -422,7 +422,7 @@
     step = 16 if rows % 16 == 0 else rows
     lanes = lax.broadcasted_iota(jnp.int32, (rows, LANES), 1)
 
-    @pl.loop(0, nsrc, unroll=2)
+    @pl.loop(0, nsrc, unroll=4)
     def _(source):
         for place in range(nblock):
             block = order_ref[source * nblock + place]

time: 146 us -> 146 us (level)
  no operation moved by 1% of the time
where the time goes in v3:
time: 146 us; the launch traced here: 145 us
  Pallas kernels  77.7 us (53%)
  waiting for transfers between devices  34.9 us (24%)
  starting transfers between devices  28.5 us (20%)
  local copies, waits for them, and re-layouts  1.59 us (1%)
  between operations  1.48 us (1%)
    ppermute x14, waiting for transfers between devices, exchange(): return lax.ppermute(x, axis, [(a, a ^ flip) for a in range(size)])  34.9 us
    pallas_call x2, Pallas kernels, left_products(): pl.pallas_call(functools.partial(left_kernel, nshard, first), grid_spec=p...  33.2 us
    ppermute x14, starting transfers between devices, exchange(): return lax.ppermute(x, axis, [(a, a ^ flip) for a in range(size)])  17.9 us
    pallas_call x2, Pallas kernels, tiles(): pl.pallas_call(functools.partial(tile_kernel, nshard, first, packed), gri...  17.9 us
    pallas_call x2, Pallas kernels, project(): pl.pallas_call(functools.partial(project_kernel, started), grid_spec=pltp...  13.7 us
    pallas_call x1, Pallas kernels, unpack(): pl.pallas_call(functools.partial(unpack_kernel, cut), grid_spec=pltpu.Pre...  7.29 us
    all_to_all x1, starting transfers between devices, body(): lax.all_to_all(tiles_a, 'src', split_axis=0, concat_axis=0, tiled=True)  6.02 us
    all_to_all x1, starting transfers between devices, body(): lax.all_to_all(packed, 'src', split_axis=0, concat_axis=0, tiled=True)  4.54 us
  transfers between devices with their start and end apart: 16, of which 7 were waited for; matrix products, arithmetic and copies ran while one was open for 1% of the time, Pallas kernels for 42%

profile of v3, /device:TPU:0, one launch (start us, length us, event | category | flops | bytes accessed | tf_op | source)
XLA Modules:
  0.0 145.2 jit_solution(10621101696377822277)
XLA Ops:
  0.6 2.8 %shard_map.94 = (s32[8]{0:T(128)}, s32[8]{0:T(128)}, bf16[3,256,384]{2,1,0:T(8,128)(2,1)}, bf16[5,256,384]{2,1,0:T(8,128)(2,1)}) custom-call(s32[8]{0:T(128)} %refs_0_.1, bf16[8,256,384]{2,1,0:T(8,128)(2,1)} %basis_ref.3), custom_call_target="tpu_custom_call" | custom-call | tf_op jit(solution)/shard_map/pallas_call | solution.py:85
  3.4 3.0 %collective-permute-start = (bf16[3,256,384]{2,1,0:T(8,128)(2,1)}, bf16[3,256,384]{2,1,0:T(8,128)(2,1)}, u32[]{:S(2)}, u32[]{:S(2)}) collective-permute-start(bf16[3,256,384]{2,1,0:T(8,128)(2,1)} %get-tuple-element.147.refs_5_), channel_id=1, source_target_pairs={{0,16},{8,24},{16,0},{24,8},{1,17},{9,25},{17,1},{25,9},{2,18},{10... | collective-permute-start | bytes 1769480 | tf_op jit(solution)/shard_map/ppermute | solution.py:19
  6.5 0.0 collective-permute-start.2
  6.5 13.5 %shard_map.95.refs_4_ = bf16[2,3,384,1024]{3,2,1,0:T(8,128)(2,1)} custom-call(s32[1]{0:T(128)} %bitcast.1.me_ref, s32[8]{0:T(128)} %get-tuple-element.144.order_ref.refs_0_, f32[3,2,1024]{2,1,0:T(2,128)} %bitcast.23, f32[3,8,1024]{2,1,0:T(8,128)} %bitcast.21, bf16[2,1024,384]{2,1,0:T(8,128)(2,1)} %basis_ref.5), custom_call_target="tpu_custom_call" | custom-call | flops 4831838208 | bytes 4718592 | tf_op jit(solution)/shard_map/pallas_call | solution.py:213
  20.0 0.2 collective-permute-done.refs_7_
  20.1 0.3 collective-permute-start.3
  20.5 0.0 collective-permute-done.2.refs_6_
  20.5 2.0 %collective-permute-done.3.refs_8_ = bf16[3,256,384]{2,1,0:T(8,128)(2,1)} collective-permute-done((bf16[3,256,384]{2,1,0:T(8,128)(2,1)}, bf16[3,256,384]{2,1,0:T(8,128)(2,1)}, u32[]{:S(2)}, u32[]{:S(2)}) %collective-permute-start.3) | collective-permute-done | bytes 589856 | tf_op jit(solution)/shard_map/ppermute | solution.py:19
  22.5 6.9 %shard_map.96.tile_ref = bf16[8,2,3,48,384]{4,3,2,1,0:T(8,128)(2,1)} custom-call(s32[8]{0:T(128)} %get-tuple-element.144.order_ref.refs_0_, s32[8]{0:T(128)} %refs_0_.1, s32[8]{0:T(128)} %get-tuple-element.145.refs_2_, s32[2]{0:T(128)} %refs_3_.3, bf16[2,3,384,1024]{3,2,1,0:T(8,128)(2,1)} %shard_map.95.refs_4_, ...), custom_call_target="tpu_custom_call" | custom-call | flops 1811939328 | bytes 6488064 | tf_op jit(solution)/shard_map/pallas_call | solution.py:321
  29.4 6.0 %all-to-all-start.3 = ((bf16[8,2,3,48,384]{4,3,2,1,0:T(8,128)(2,1)}), bf16[8,2,3,48,384]{4,3,2,1,0:T(8,128)(2,1)}, u32[]{:S(2)}, u32[]{:S(2)}) async-start(bf16[8,2,3,48,384]{4,3,2,1,0:T(8,128)(2,1)} %shard_map.96.tile_ref), calls=%async_computation.3 | async-start | bytes 3538944 | tf_op jit(solution)/shard_map/all_to_all | solution.py:522
  35.4 1.6 %collective-permute-start.1 = (bf16[5,256,384]{2,1,0:T(8,128)(2,1)}, bf16[5,256,384]{2,1,0:T(8,128)(2,1)}, u32[]{:S(2)}, u32[]{:S(2)}) collective-permute-start(bf16[5,256,384]{2,1,0:T(8,128)(2,1)} %get-tuple-element.148.refs_5_), channel_id=1, source_target_pairs={{0,16},{8,24},{16,0},{24,8},{1,17},{9,25},{17,1},{25,9},{2,18},{10... | collective-permute-start | bytes 2949128 | tf_op jit(solution)/shard_map/ppermute | solution.py:19
  37.0 0.0 collective-permute-start.4
  37.0 19.7 %shard_map.97.refs_4_ = bf16[2,5,384,1024]{3,2,1,0:T(8,128)(2,1)} custom-call(s32[1]{0:T(128)} %bitcast.1.me_ref, s32[8]{0:T(128)} %get-tuple-element.144.order_ref.refs_0_, f32[3,2,1024]{2,1,0:T(2,128)} %bitcast.24, f32[3,8,1024]{2,1,0:T(8,128)} %bitcast.22, bf16[2,1024,384]{2,1,0:T(8,128)(2,1)} %basis_ref.5), custom_call_target="tpu_custom_call" | custom-call | flops 8053063680 | bytes 7864320 | tf_op jit(solution)/shard_map/pallas_call | solution.py:213
  56.7 2.6 %collective-permute-done.1.refs_7_ = bf16[5,256,384]{2,1,0:T(8,128)(2,1)} collective-permute-done((bf16[5,256,384]{2,1,0:T(8,128)(2,1)}, bf16[5,256,384]{2,1,0:T(8,128)(2,1)}, u32[]{:S(2)}, u32[]{:S(2)}) %collective-permute-start.1) | collective-permute-done | bytes 983072 | tf_op jit(solution)/shard_map/ppermute | solution.py:19
  59.3 0.0 collective-permute-start.5
  59.3 0.0 copy-done
  59.3 1.7 %collective-permute-start.6 = (s32[8]{0:T(128)S(1)}, s32[8]{0:T(128)S(1)}, u32[]{:S(2)}, u32[]{:S(2)}) collective-permute-start(s32[8]{0:T(128)S(1)} %copy-done), channel_id=1, source_target_pairs={{0,2},{1,3},{2,0},{3,1},{4,6},{5,7},{6,4},{7,5},{8,10},{9,11},{10,... | collective-permute-start | bytes 104 | tf_op jit(solution)/shard_map/ppermute | solution.py:19
  61.0 2.4 %collective-permute-start.7 = (s32[8]{0:T(128)S(1)}, s32[8]{0:T(128)S(1)}, u32[]{:S(2)}, u32[]{:S(2)}) collective-permute-start(s32[8]{0:T(128)S(1)} %copy-done), channel_id=1, source_target_pairs={{0,4},{1,5},{2,6},{3,7},{4,0},{5,1},{6,2},{7,3},{8,12},{9,13},{10,... | collective-permute-start | bytes 104 | tf_op jit(solution)/shard_map/ppermute | solution.py:19
  63.3 0.3 collective-permute-start.8
  63.7 0.0 collective-permute-done.4.refs_6_
  63.7 0.0 collective-permute-done.5.refs_8_
  63.7 11.0 %shard_map.98 = (bf16[8,2,5,48,384]{4,3,2,1,0:T(8,128)(2,1)}, bf16[8,2,48,1408]{3,2,1,0:T(8,128)(2,1)}, bf16[8,2,48,512]{3,2,1,0:T(8,128)(2,1)}) custom-call(s32[8]{0:T(128)} %get-tuple-element.144.order_ref.refs_0_, s32[8]{0:T(128)} %refs_0_.1, s32[8]{0:T(128)} %get-tuple-element.145.refs_2_, s32[2]{0:T(128)} %refs_3_.3, ...), custom_call_target="tpu_custom_call" | custom-call | flops 3019898880 | bytes 10813440 | tf_op jit(solution)/shard_map/pallas_call | solution.py:321
  74.7 0.0 collective-permute-done.6.refs_1_
  74.7 0.0 copy-start.1
  74.7 2.3 %collective-permute-done.7.refs_2_ = s32[8]{0:T(128)S(1)} collective-permute-done((s32[8]{0:T(128)S(1)}, s32[8]{0:T(128)S(1)}, u32[]{:S(2)}, u32[]{:S(2)}) %collective-permute-start.7) | collective-permute-done | bytes 64 | tf_op jit(solution)/shard_map/ppermute | solution.py:19
  77.0 0.0 collective-permute-done.8.refs_3_
  77.1 0.0 all-to-all-done.3
  77.1 4.5 %all-to-all-start.4 = ((bf16[8,2,48,1408]{3,2,1,0:T(8,128)(2,1)}), bf16[8,2,48,1408]{3,2,1,0:T(8,128)(2,1)}, u32[]{:S(2)}, u32[]{:S(2)}) async-start(bf16[8,2,48,1408]{3,2,1,0:T(8,128)(2,1)} %get-tuple-element.156), calls=%async_computation.4 | async-start | bytes 4325376 | tf_op jit(solution)/shard_map/all_to_all | solution.py:533
  81.6 0.0 copy-done.1
  81.7 5.7 %shard_map.99 = (f32[768,512]{1,0:T(8,128)}, s32[32]{0:T(128)}) custom-call(s32[8]{0:T(128)} %get-tuple-element.144.order_ref.refs_0_, bf16[8,2,3,48,384]{4,3,2,1,0:T(8,128)(2,1)} %shard_map.96.tile_ref, bf16[8,384,512]{2,1,0:T(8,128)(2,1)} %coeff_ref.3, s32[8]{0:T(128)} %refs_0_.1, s32[8]{0:T(128)} %copy-done.1, s32[8]{0:T(128)} %copy-done.2, s32[8]{0:T(128)} %copy-done.3), custom_call_target="tpu_custom_call" | custom-call | flops 905969664 | bytes 1769472 | tf_op jit(solution)/shard_map/pallas_call | solution.py:391
  87.4 7.9 %shard_map.101 = bf16[8,2,48,512]{3,2,1,0:T(8,128)(2,1)} custom-call(s32[8]{0:T(128)} %get-tuple-element.144.order_ref.refs_0_, bf16[8,2,5,48,384]{4,3,2,1,0:T(8,128)(2,1)} %get-tuple-element.166.tile_ref, bf16[8,384,512]{2,1,0:T(8,128)(2,1)} %coeff_ref.3, f32[768,512]{1,0:T(8,128)} %get-tuple-element.167.refs_0_), custom_call_target="tpu_custom_call" | custom-call | flops 1509949440 | bytes 2949120 | tf_op jit(solution)/shard_map/pallas_call | solution.py:391
  95.4 1.0 dynamic-slice_bitcast_fusion
  96.4 1.7 %collective-permute-start.10 = (bf16[4,2,48,512]{3,2,1,0:T(8,128)(2,1)S(1)}, bf16[4,2,48,512]{3,2,1,0:T(8,128)(2,1)S(1)}, u32[]{:S(2)}, u32[]{:S(2)}) collective-permute-start(bf16[4,2,48,512]{3,2,1,0:T(8,128)(2,1)S(1)} %dynamic-slice_bitcast_fusion), channel_id=1, source_target_pairs={{0,1},{1,0},{2,3},{3,2},{4,5},{5,4},{6,7},{7,6},{8,9},{9,8},{10,11... | collective-permute-start | bytes 1179656 | tf_op jit(solution)/shard_map/ppermute | solution.py:19
  98.1 18.7 %collective-permute-done.10 = bf16[4,2,48,512]{3,2,1,0:T(8,128)(2,1)S(1)} collective-permute-done((bf16[4,2,48,512]{3,2,1,0:T(8,128)(2,1)S(1)}, bf16[4,2,48,512]{3,2,1,0:T(8,128)(2,1)S(1)}, u32[]{:S(2)}, u32[]{:S(2)}) %collective-permute-start.10) | collective-permute-done | bytes 393248 | tf_op jit(solution)/shard_map/ppermute | solution.py:19
  116.8 1.1 fusion
  118.0 0.1 collective-permute-start.11
  118.1 6.7 %collective-permute-start.12 = (bf16[2,48,512]{2,1,0:T(8,128)(2,1)S(1)}, bf16[2,48,512]{2,1,0:T(8,128)(2,1)S(1)}, u32[]{:S(2)}, u32[]{:S(2)}) collective-permute-start(bf16[2,48,512]{2,1,0:T(8,128)(2,1)S(1)} %get-tuple-element.180), channel_id=1, source_target_pairs={{0,4},{1,5},{2,6},{3,7},{4,0},{5,1},{6,2},{7,3},{8,12},{9,13},{10,... | collective-permute-start | bytes 294920 | tf_op jit(solution)/shard_map/ppermute | solution.py:19
  124.8 0.0 collective-permute-start.13
  124.8 0.0 collective-permute-start.9
  124.8 3.5 %collective-permute-done.9.refs_1_ = s32[32]{0:T(128)S(1)} collective-permute-done((s32[32]{0:T(128)S(1)}, s32[32]{0:T(128)S(1)}, u32[]{:S(2)}, u32[]{:S(2)}) %collective-permute-start.9) | collective-permute-done | bytes 160 | tf_op jit(solution)/shard_map/ppermute | solution.py:19
  128.3 0.5 copy-done.5
  128.9 2.8 %shard_map.100 = (s32[64]{0:T(128)S(1)}, s32[64]{0:T(128)S(1)}, s32[64]{0:T(128)S(1)}, s32[1]{0:T(128)}) custom-call(s32[1]{0:T(128)} %bitcast.me_ref, s32[32]{0:T(128)} %get-tuple-element.161.refs_0_, s32[32]{0:T(128)} %copy-done.5), custom_call_target="tpu_custom_call" | custom-call | tf_op jit(solution)/shard_map/pallas_call | solution.py:131
  132.3 0.0 collective-permute-done.11
  132.3 5.6 %collective-permute-done.12 = bf16[2,48,512]{2,1,0:T(8,128)(2,1)S(1)} collective-permute-done((bf16[2,48,512]{2,1,0:T(8,128)(2,1)S(1)}, bf16[2,48,512]{2,1,0:T(8,128)(2,1)S(1)}, u32[]{:S(2)}, u32[]{:S(2)}) %collective-permute-start.12) | collective-permute-done | bytes 98336 | tf_op jit(solution)/shard_map/ppermute | solution.py:19
  137.9 0.0 collective-permute-done.13
  137.9 0.0 all-to-all-done.4
  137.9 7.3 %conditional.1 = ((bf16[2,48,64,384]{3,2,1,0:T(8,128)(2,1)}, bf16[2,48,512]{2,1,0:T(8,128)(2,1)})) conditional(s32[]{:T(128)} %bitcast.4, (s32[64]{0:T(128)S(1)}, s32[64]{0:T(128)S(1)}, s32[64]{0:T(128)S(1)}, bf16[8,2,3,48,384]{4,3,2,1,0:T(8,128)(2,1)}, bf16[8,2,48,1408]{3,2,1,0:T(8,128)(2,1)}, ...), branch_computations={%region_0.1_spmd, %region_1.2_spmd, %region_2.3_spmd, %region_3.4_... | conditional | flops 5898240 | bytes 7471112 | solution.py:551
  137.9 7.3 %branch_0_fun.1 = (bf16[2,48,64,384]{3,2,1,0:T(8,128)(2,1)}, bf16[2,48,512]{2,1,0:T(8,128)(2,1)}) custom-call(s32[64]{0:T(128)S(1)} %get-tuple-element.78.order_ref, s32[64]{0:T(128)S(1)} %get-tuple-element.79.counts_ref, s32[64]{0:T(128)S(1)} %get-tuple-element.80.offsets_ref, bf16[8,2,3,48,384]{4,3,2,1,0:T(8,128)(2,1)} %get-tuple-element.81.whole_ref, ...), custom_call_target="tpu_custom_call" | custom-call | tf_op jit(solution)/shard_map/cond/branch_0_fun/pallas_call | solution.py:462
  (9 shorter events, 0.1 us)
Async XLA Ops:
  3.4 16.7 %collective-permute-start = (bf16[3,256,384]{2,1,0:T(8,128)(2,1)}, bf16[3,256,384]{2,1,0:T(8,128)(2,1)}, u32[]{:S(2)}, u32[]{:S(2)}) collective-permute-start(bf16[3,256,384]{2,1,0:T(8,128)(2,1)} %get-tuple-element.147.refs_5_), channel_id=1, source_target_pairs={{0,16},{8,24},{16,0},{24,8},{1,17},{9,25},{17,1},{25,9},{2,18},{10... | collective-permute-start | bytes 1769480 | tf_op jit(solution)/shard_map/ppermute | solution.py:19
  6.5 14.0 %collective-permute-start.2 = (bf16[3,256,384]{2,1,0:T(8,128)(2,1)}, bf16[3,256,384]{2,1,0:T(8,128)(2,1)}, u32[]{:S(2)}, u32[]{:S(2)}) collective-permute-start(bf16[3,256,384]{2,1,0:T(8,128)(2,1)} %get-tuple-element.147.refs_5_), channel_id=1, source_target_pairs={{0,8},{8,0},{16,24},{24,16},{1,9},{9,1},{17,25},{25,17},{2,10},{10... | collective-permute-start | bytes 1769480 | tf_op jit(solution)/shard_map/ppermute | solution.py:19
  20.1 2.3 %collective-permute-start.3 = (bf16[3,256,384]{2,1,0:T(8,128)(2,1)}, bf16[3,256,384]{2,1,0:T(8,128)(2,1)}, u32[]{:S(2)}, u32[]{:S(2)}) collective-permute-start(bf16[3,256,384]{2,1,0:T(8,128)(2,1)} %collective-permute-done.refs_7_), channel_id=1, source_target_pairs={{0,8},{8,0},{16,24},{24,16},{1,9},{9,1},{17,25},{25,17},{2,10},{10... | collective-permute-start | bytes 1769480 | tf_op jit(solution)/shard_map/ppermute | solution.py:19
  29.4 47.7 %all-to-all-start.3 = ((bf16[8,2,3,48,384]{4,3,2,1,0:T(8,128)(2,1)}), bf16[8,2,3,48,384]{4,3,2,1,0:T(8,128)(2,1)}, u32[]{:S(2)}, u32[]{:S(2)}) async-start(bf16[8,2,3,48,384]{4,3,2,1,0:T(8,128)(2,1)} %shard_map.96.tile_ref), calls=%async_computation.3 | async-start | bytes 3538944 | tf_op jit(solution)/shard_map/all_to_all | solution.py:522
  35.4 23.9 %copy-start = (s32[8]{0:T(128)S(1)}, s32[8]{0:T(128)}, u32[]{:S(2)}) copy-start(s32[8]{0:T(128)} %refs_0_.1) | copy-start | bytes 100
  35.4 23.9 %collective-permute-start.1 = (bf16[5,256,384]{2,1,0:T(8,128)(2,1)}, bf16[5,256,384]{2,1,0:T(8,128)(2,1)}, u32[]{:S(2)}, u32[]{:S(2)}) collective-permute-start(bf16[5,256,384]{2,1,0:T(8,128)(2,1)} %get-tuple-element.148.refs_5_), channel_id=1, source_target_pairs={{0,16},{8,24},{16,0},{24,8},{1,17},{9,25},{17,1},{25,9},{2,18},{10... | collective-permute-start | bytes 2949128 | tf_op jit(solution)/shard_map/ppermute | solution.py:19
  37.0 26.7 %collective-permute-start.4 = (bf16[5,256,384]{2,1,0:T(8,128)(2,1)}, bf16[5,256,384]{2,1,0:T(8,128)(2,1)}, u32[]{:S(2)}, u32[]{:S(2)}) collective-permute-start(bf16[5,256,384]{2,1,0:T(8,128)(2,1)} %get-tuple-element.148.refs_5_), channel_id=1, source_target_pairs={{0,8},{8,0},{16,24},{24,16},{1,9},{9,1},{17,25},{25,17},{2,10},{10... | collective-permute-start | bytes 2949128 | tf_op jit(solution)/shard_map/ppermute | solution.py:19
  59.3 4.4 %collective-permute-start.5 = (bf16[5,256,384]{2,1,0:T(8,128)(2,1)}, bf16[5,256,384]{2,1,0:T(8,128)(2,1)}, u32[]{:S(2)}, u32[]{:S(2)}) collective-permute-start(bf16[5,256,384]{2,1,0:T(8,128)(2,1)} %collective-permute-done.1.refs_7_), channel_id=1, source_target_pairs={{0,8},{8,0},{16,24},{24,16},{1,9},{9,1},{17,25},{25,17},{2,10},{10... | collective-permute-start | bytes 2949128 | tf_op jit(solution)/shard_map/ppermute | solution.py:19
  59.3 15.4 %collective-permute-start.6 = (s32[8]{0:T(128)S(1)}, s32[8]{0:T(128)S(1)}, u32[]{:S(2)}, u32[]{:S(2)}) collective-permute-start(s32[8]{0:T(128)S(1)} %copy-done), channel_id=1, source_target_pairs={{0,2},{1,3},{2,0},{3,1},{4,6},{5,7},{6,4},{7,5},{8,10},{9,11},{10,... | collective-permute-start | bytes 104 | tf_op jit(solution)/shard_map/ppermute | solution.py:19
  61.0 16.1 %collective-permute-start.7 = (s32[8]{0:T(128)S(1)}, s32[8]{0:T(128)S(1)}, u32[]{:S(2)}, u32[]{:S(2)}) collective-permute-start(s32[8]{0:T(128)S(1)} %copy-done), channel_id=1, source_target_pairs={{0,4},{1,5},{2,6},{3,7},{4,0},{5,1},{6,2},{7,3},{8,12},{9,13},{10,... | collective-permute-start | bytes 104 | tf_op jit(solution)/shard_map/ppermute | solution.py:19
  63.3 13.7 %collective-permute-start.8 = (s32[8]{0:T(128)S(1)}, s32[8]{0:T(128)S(1)}, u32[]{:S(2)}, u32[]{:S(2)}) collective-permute-start(s32[8]{0:T(128)S(1)} %copy-done), channel_id=1, source_target_pairs={{0,6},{1,7},{2,4},{3,5},{4,2},{5,3},{6,0},{7,1},{8,14},{9,15},{10,... | collective-permute-start | bytes 104 | tf_op jit(solution)/shard_map/ppermute | solution.py:19
  74.7 6.9 %copy-start.1 = (s32[8]{0:T(128)}, s32[8]{0:T(128)S(1)}, u32[]{:S(2)}) copy-start(s32[8]{0:T(128)S(1)} %collective-permute-done.6.refs_1_) | copy-start | bytes 100
  77.0 4.6 %copy-start.2 = (s32[8]{0:T(128)}, s32[8]{0:T(128)S(1)}, u32[]{:S(2)}) copy-start(s32[8]{0:T(128)S(1)} %collective-permute-done.7.refs_2_) | copy-start | bytes 100
  77.0 4.6 %copy-start.3 = (s32[8]{0:T(128)}, s32[8]{0:T(128)S(1)}, u32[]{:S(2)}) copy-start(s32[8]{0:T(128)S(1)} %collective-permute-done.8.refs_3_) | copy-start | bytes 100
  77.1 60.9 %all-to-all-start.4 = ((bf16[8,2,48,1408]{3,2,1,0:T(8,128)(2,1)}), bf16[8,2,48,1408]{3,2,1,0:T(8,128)(2,1)}, u32[]{:S(2)}, u32[]{:S(2)}) async-start(bf16[8,2,48,1408]{3,2,1,0:T(8,128)(2,1)} %get-tuple-element.156), calls=%async_computation.4 | async-start | bytes 4325376 | tf_op jit(solution)/shard_map/all_to_all | solution.py:533
  87.4 37.4 %copy-start.4 = (s32[32]{0:T(128)S(1)}, s32[32]{0:T(128)}, u32[]{:S(2)}) copy-start(s32[32]{0:T(128)} %get-tuple-element.161.refs_0_) | copy-start | bytes 388
  96.4 20.4 %collective-permute-start.10 = (bf16[4,2,48,512]{3,2,1,0:T(8,128)(2,1)S(1)}, bf16[4,2,48,512]{3,2,1,0:T(8,128)(2,1)S(1)}, u32[]{:S(2)}, u32[]{:S(2)}) collective-permute-start(bf16[4,2,48,512]{3,2,1,0:T(8,128)(2,1)S(1)} %dynamic-slice_bitcast_fusion), channel_id=1, source_target_pairs={{0,1},{1,0},{2,3},{3,2},{4,5},{5,4},{6,7},{7,6},{8,9},{9,8},{10,11... | collective-permute-start | bytes 1179656 | tf_op jit(solution)/shard_map/ppermute | solution.py:19
  118.0 14.4 %collective-permute-start.11 = (bf16[2,48,512]{2,1,0:T(8,128)(2,1)S(1)}, bf16[2,48,512]{2,1,0:T(8,128)(2,1)S(1)}, u32[]{:S(2)}, u32[]{:S(2)}) collective-permute-start(bf16[2,48,512]{2,1,0:T(8,128)(2,1)S(1)} %get-tuple-element.181), channel_id=1, source_target_pairs={{0,2},{1,3},{2,0},{3,1},{4,6},{5,7},{6,4},{7,5},{8,10},{9,11},{10,... | collective-permute-start | bytes 294920 | tf_op jit(solution)/shard_map/ppermute | solution.py:19
  118.1 19.9 %collective-permute-start.12 = (bf16[2,48,512]{2,1,0:T(8,128)(2,1)S(1)}, bf16[2,48,512]{2,1,0:T(8,128)(2,1)S(1)}, u32[]{:S(2)}, u32[]{:S(2)}) collective-permute-start(bf16[2,48,512]{2,1,0:T(8,128)(2,1)S(1)} %get-tuple-element.180), channel_id=1, source_target_pairs={{0,4},{1,5},{2,6},{3,7},{4,0},{5,1},{6,2},{7,3},{8,12},{9,13},{10,... | collective-permute-start | bytes 294920 | tf_op jit(solution)/shard_map/ppermute | solution.py:19
  124.8 13.1 %collective-permute-start.13 = (bf16[2,48,512]{2,1,0:T(8,128)(2,1)S(1)}, bf16[2,48,512]{2,1,0:T(8,128)(2,1)S(1)}, u32[]{:S(2)}, u32[]{:S(2)}) collective-permute-start(bf16[2,48,512]{2,1,0:T(8,128)(2,1)S(1)} %get-tuple-element.179), channel_id=1, source_target_pairs={{0,6},{1,7},{2,4},{3,5},{4,2},{5,3},{6,0},{7,1},{8,14},{9,15},{10,... | collective-permute-start | bytes 294920 | tf_op jit(solution)/shard_map/ppermute | solution.py:19
  124.8 3.5 %collective-permute-start.9 = (s32[32]{0:T(128)S(1)}, s32[32]{0:T(128)S(1)}, u32[]{:S(2)}, u32[]{:S(2)}) collective-permute-start(s32[32]{0:T(128)S(1)} %copy-done.4), channel_id=1, source_target_pairs={{0,1},{1,0},{2,3},{3,2},{4,5},{5,4},{6,7},{7,6},{8,9},{9,8},{10,11... | collective-permute-start | bytes 392 | tf_op jit(solution)/shard_map/ppermute | solution.py:19
  128.3 0.5 copy-start.5
